TPU v7x, 512 devices: a whole 4x4x16 slice. The times are simulated.
512 devices in a mesh: gx: 4 (over z_lo), gy: 8 (over z_hi, core), zt: 16 (over x, y).
Axes of the slice: x: 4, y: 4, z: 16 (z_hi: 4, z_lo: 4; z = z_hi * 4 + z_lo), core: 2. Of those that a mesh axis runs over, the one named last changes fastest.
Arguments:
- near_null: bfloat16 [16, 32, 64, 2, 1152], P('gx', 'gy', 'zt'), may hold values from -6 to 6
- gauge: bfloat16 [16, 32, 64, 2, 144], P('gx', 'gy', 'zt'), may hold values from -6 to 6
- site_map: int32 [16, 32], P('zt'), may hold values from 0 to 31, each once within a row
Outputs:
- coarse_links: float32 [16, 32, 2, 9216], P('zt')
Inputs may be any that keep to these rules, and one draw needn't show every extreme that they name: Each row of site_map names every coarse site 0 to 31 once.
All inputs are finite; a program needn't handle non-finite values.
Results may differ from a plain program's by a relative error of at most 0.0004.
Values may be sent and summed in bfloat16 or wider, within the bound.
No kernel may reach another device: no remote copies, remote signals or barrier semaphores. Data moves between devices by JAX's collectives and lax.ppermute only.
A program may use at most 64 MiB of HBM per device.

v0:
```python
import jax
import jax.numpy as jnp
import numpy as np
from jax import lax
from jax.sharding import PartitionSpec as P


def passed_along(value, axis, steps):
    count = lax.axis_size(axis)
    pairs = [(source, (source + steps) % count) for source in range(count)]
    return lax.ppermute(value, axis, pairs)


def spin_blocks():
    nought = np.zeros((2, 2))
    return [
        (nought, np.array([[0.0, -1.0], [-1.0, 0.0]])),
        (np.array([[0.0, -1.0], [1.0, 0.0]]), nought),
        (nought, np.array([[-1.0, 0.0], [0.0, 1.0]])),
        (np.eye(2), nought),
    ]


def chiral_layout(block):
    extent = block.shape[0]
    count = block.shape[-1] // (extent * 12)
    shaped = block.reshape(extent, extent, extent, 2, extent, 2, 2, 3, count)
    return jnp.transpose(shaped, (5, 3, 8, 7, 6, 0, 1, 2, 4))


def gauge_layout(block):
    extent = block.shape[0]
    shaped = block.reshape(extent, extent, extent, 2, 4, extent, 3, 3)
    return jnp.transpose(shaped, (4, 3, 6, 7, 0, 1, 2, 5)).astype(jnp.float32)


def gram_of(flat):
    flat_re = flat[:, 0]
    flat_im = flat[:, 1]
    gram_re = jnp.einsum(
        "nkr,nlr->nkl", flat_re, flat_re, preferred_element_type=jnp.float32
    ) + jnp.einsum("nkr,nlr->nkl", flat_im, flat_im, preferred_element_type=jnp.float32)
    gram_im = jnp.einsum(
        "nkr,nlr->nkl", flat_re, flat_im, preferred_element_type=jnp.float32
    ) - jnp.einsum("nkr,nlr->nkl", flat_im, flat_re, preferred_element_type=jnp.float32)
    return jnp.stack([gram_re, gram_im], axis=1)


def coefficients(gram_matrix, target):
    highest = lax.Precision.HIGHEST
    vector_count = gram_matrix.shape[-1]
    identity = jnp.eye(vector_count, dtype=gram_matrix.dtype)
    gram_re = gram_matrix[:, 0]
    gram_im = gram_matrix[:, 1]

    def gram_step(column, mixing):
        picked = lax.dynamic_index_in_dim(gram_matrix, column, 3, keepdims=False)
        unit_column = lax.dynamic_index_in_dim(identity, column, 1, keepdims=False)
        mixing_re = mixing[:, 0]
        mixing_im = mixing[:, 1]
        picked_re = picked[:, 0]
        picked_im = picked[:, 1]
        project_re = jnp.einsum("nlk,nl->nk", mixing_re, picked_re, precision=highest) + jnp.einsum(
            "nlk,nl->nk", mixing_im, picked_im, precision=highest
        )
        project_im = jnp.einsum("nlk,nl->nk", mixing_re, picked_im, precision=highest) - jnp.einsum(
            "nlk,nl->nk", mixing_im, picked_re, precision=highest
        )
        remain_re = unit_column - (
            jnp.einsum("nlk,nk->nl", mixing_re, project_re, precision=highest)
            - jnp.einsum("nlk,nk->nl", mixing_im, project_im, precision=highest)
        )
        remain_im = -(
            jnp.einsum("nlk,nk->nl", mixing_re, project_im, precision=highest)
            + jnp.einsum("nlk,nk->nl", mixing_im, project_re, precision=highest)
        )
        image_re = jnp.einsum("nlk,nk->nl", gram_re, remain_re, precision=highest) - jnp.einsum(
            "nlk,nk->nl", gram_im, remain_im, precision=highest
        )
        image_im = jnp.einsum("nlk,nk->nl", gram_re, remain_im, precision=highest) + jnp.einsum(
            "nlk,nk->nl", gram_im, remain_re, precision=highest
        )
        weight = jnp.sum(remain_re * image_re + remain_im * image_im, axis=-1)
        factor = jnp.sqrt(target / weight)
        new_column = jnp.stack([remain_re, remain_im], axis=1) * factor[:, None, None]
        return mixing + new_column[..., None] * unit_column

    return lax.fori_loop(0, vector_count, gram_step, jnp.zeros_like(gram_matrix))


def combine(flat, mixing):
    highest = lax.Precision.HIGHEST
    widened = flat.astype(jnp.float32)
    flat_re = widened[:, 0]
    flat_im = widened[:, 1]
    mixing_re = mixing[:, 0]
    mixing_im = mixing[:, 1]
    result_re = jnp.einsum("nlk,nlr->nkr", mixing_re, flat_re, precision=highest) - jnp.einsum(
        "nlk,nlr->nkr", mixing_im, flat_im, precision=highest
    )
    result_im = jnp.einsum("nlk,nlr->nkr", mixing_re, flat_im, precision=highest) + jnp.einsum(
        "nlk,nlr->nkr", mixing_im, flat_re, precision=highest
    )
    return jnp.stack([result_re, result_im], axis=1)


def orthonormalize(vectors):
    extent = vectors.shape[-1]
    flat = vectors.reshape(vectors.shape[:3] + (-1,))
    mixing = coefficients(gram_of(flat), extent**3)
    return (combine(flat, mixing).reshape(vectors.shape), mixing)


def boundary_face(basis, position, layer):
    sliced = lax.index_in_dim(basis, layer, 5 + position, keepdims=False)
    return sliced.reshape(sliced.shape[:4] + (-1,))


def link_face(links, direction, layer):
    sliced = lax.index_in_dim(links[direction], layer, 3 + direction, keepdims=False)
    flat = sliced.reshape(sliced.shape[:3] + (-1,))
    return jnp.concatenate([flat, flat], axis=-1)


def apply_spin(matrix_re, matrix_im, value_re, value_im):
    halfway = value_re.shape[-1] // 2
    parts_re = [value_re[..., :halfway], value_re[..., halfway:]]
    parts_im = [value_im[..., :halfway], value_im[..., halfway:]]
    outs_re = []
    outs_im = []
    for row_spin in range(2):
        total_re = jnp.zeros_like(parts_re[0])
        total_im = jnp.zeros_like(parts_im[0])
        for col_spin in range(2):
            coef_re = float(matrix_re[row_spin, col_spin])
            coef_im = float(matrix_im[row_spin, col_spin])
            if coef_re != 0.0:
                total_re = total_re + coef_re * parts_re[col_spin]
                total_im = total_im + coef_re * parts_im[col_spin]
            if coef_im != 0.0:
                total_re = total_re - coef_im * parts_im[col_spin]
                total_im = total_im + coef_im * parts_re[col_spin]
        outs_re.append(total_re)
        outs_im.append(total_im)
    return (jnp.concatenate(outs_re, axis=-1), jnp.concatenate(outs_im, axis=-1))


def inner_block(left_re, left_im, right_re, right_im):
    highest = lax.Precision.HIGHEST
    count = left_re.shape[0]
    left_re = left_re.reshape(count, -1)
    left_im = left_im.reshape(count, -1)
    right_re = right_re.reshape(count, -1)
    right_im = right_im.reshape(count, -1)
    result_re = jnp.einsum("kr,lr->kl", left_re, right_re, precision=highest) + jnp.einsum(
        "kr,lr->kl", left_im, right_im, precision=highest
    )
    result_im = jnp.einsum("kr,lr->kl", left_re, right_im, precision=highest) - jnp.einsum(
        "kr,lr->kl", left_im, right_re, precision=highest
    )
    return (result_re, result_im)


def coarse_link(own_face, after_face, hopping, direction):
    after_re = after_face[:, 0][:, :, None]
    after_im = after_face[:, 1][:, :, None]
    link_re = hopping[0][None, None]
    link_im = hopping[1][None, None]
    moved_re = jnp.sum(link_re * after_re, axis=3) - jnp.sum(link_im * after_im, axis=3)
    moved_im = jnp.sum(link_re * after_im, axis=3) + jnp.sum(link_im * after_re, axis=3)
    matrix_re, matrix_im = spin_blocks()[direction]
    upper_re, upper_im = apply_spin(matrix_re, matrix_im, moved_re[1], moved_im[1])
    lower_re, lower_im = apply_spin(matrix_re.T, -matrix_im.T, moved_re[0], moved_im[0])
    own_re = own_face[:, 0]
    own_im = own_face[:, 1]
    same_zero = inner_block(own_re[0], own_im[0], moved_re[0], moved_im[0])
    same_one = inner_block(own_re[1], own_im[1], moved_re[1], moved_im[1])
    cross_up = inner_block(own_re[0], own_im[0], upper_re, upper_im)
    cross_down = inner_block(own_re[1], own_im[1], lower_re, lower_im)
    parts = []
    for member in range(2):
        top = jnp.concatenate([same_zero[member], -cross_up[member]], axis=1)
        bottom = jnp.concatenate([-cross_down[member], same_one[member]], axis=1)
        parts.append(jnp.concatenate([top, bottom], axis=0))
    return jnp.stack(parts)


def block_links(basis, far_faces, links):
    extent = basis.shape[-1]
    result = []
    for direction in range(4):
        own_face = boundary_face(basis, direction, extent - 1)
        hopping = link_face(links, direction, extent - 1)
        if direction < 3:
            after_face = far_faces[direction]
        else:
            after_face = -boundary_face(basis, 3, 0)
        result.append(coarse_link(own_face, after_face, hopping, direction))
    stacked = jnp.stack(result, axis=1)
    return stacked.reshape(2, -1)


def body(near_null, gauge, site_map):
    vectors = chiral_layout(near_null)
    links = gauge_layout(gauge)
    prolong, mixing = orthonormalize(vectors)
    after_x = passed_along(boundary_face(prolong, 0, 0), "gx", -1)
    after_y = passed_along(boundary_face(prolong, 1, 0), "gy", -1)
    after_z = passed_along(boundary_face(prolong, 2, 0), "zt", -1)
    far_faces = [after_x, after_y, after_z]
    coarse_block = block_links(prolong, far_faces, links)[None]
    gathered = lax.all_gather(coarse_block, ("gx", "gy"), axis=0, tiled=True)
    placed = jnp.zeros_like(gathered).at[site_map[0]].set(gathered)
    return placed[None]


def solution(mesh):
    return jax.shard_map(
        body,
        mesh=mesh,
        in_specs=(P("gx", "gy", "zt", None, None), P("gx", "gy", "zt", None, None), P("zt", None)),
        out_specs=P("zt", None, None, None),
        check_vma=False,
    )
```

profile of v0, /device:TPU:39, one launch (start us, length us, event | category | flops | bytes accessed | tf_op | source)
XLA Modules:
  0.0 340.3 jit_solution(18045760598321426513)
XLA Ops:
  6.5 5.0 %reshape.170 = bf16[4,4,4,2,4,2,2,3,24]{8,7,6,5,4,3,2,1,0:T(4,128)(2,1)} reshape(bf16[4,4,4,2,1152]{4,3,2,1,0:T(2,128)(2,1)} %param.5) | data formatting | bytes 589824 | tf_op jit(solution)/shard_map/reshape | solution.py:27
  11.6 2.5 copy.181
  15.6 54.2 %while.14 = (s32[]{:T(128)}, f32[2,2,24,24]{3,2,1,0:T(8,128)S(1)}, f32[24,24]{0,1:T(8,128)S(1)}, f32[2,2,24,24]{2,1,0,3:T(2,128)S(1)}, f32[2,24,24]{2,1,0:T(8,12...) while((s32[]{:T(128)}, f32[2,2,24,24]{3,2,1,0:T(8,128)S(1)}, f32[24,24]{0,1:T(8,128)S(1)}, ...), condition=%wide.region_2.3_spmd.clone, body=%wide.region_0.2_spmd.clone.sunk | while | flops 175875 | bytes 269832 | solution.py:88
  72.1 1.7 copy.188
  74.5 1.6 copy.187
  76.1 1.9 copy_dynamic-update-slice_fusion.1
  78.6 1.2 fusion.198
  79.8 1.1 copy.194
  80.9 2.0 copy.195
  82.9 1.9 collective-permute-start
  84.8 1.2 fusion.199
  86.0 1.1 copy.210
  87.2 2.0 copy.211
  89.2 2.7 collective-permute-start.1
  91.9 2.9 fusion.200
  94.8 2.0 copy.225
  96.8 5.0 %collective-permute-start.2 = (f32[2,2,24,3,128]{4,2,3,1,0:T(8,128)}, f32[2,2,24,3,128]{4,2,3,1,0:T(8,128)}, u32[]{:S(2)}, u32[]{:S(2)}) collective-permute-start(f32[2,2,24,3,128]{4,2,3,1,0:T(8,128)} %copy.225), channel_id=1, source_target_pairs={{0,15},{1,0},{2,1},{3,2},{4,3},{5,4},{6,5},{7,6},{8,7},{9,8},{10,9... | collective-permute-start | bytes 442376 | tf_op jit(solution)/shard_map/ppermute | solution.py:11
  101.8 1.6 slice_negate_fusion
  103.5 5.3 %reshape.186 = f32[4,4,4,2,4,4,3,3]{7,6,5,4,3,2,1,0:T(4,128)} reshape(bf16[4,4,4,2,144]{4,3,2,1,0:T(2,128)(2,1)S(1)} %copy-done.7) | data formatting | bytes 110592 | tf_op jit(solution)/shard_map/convert_element_type | solution.py:34
  108.8 5.0 %slice_bitcast_fusion.19 = (f32[2,3,3,4,4,4,4]{2,1,6,0,5,4,3:T(4,128)}, f32[2,3,3,4,4,4,4]{2,1,6,0,5,4,3:T(4,128)S(1)}, f32[2,3,3,4,4,4,4]{2,1,6,0,5,4,3:T(4,128)}, f32[2,3,3,4,4,4,4]{2,1,6,0,5,4,3:T(4,128)S(1)}) fusion(f32[4,2,3,3,4,4,4,4]{3,2,7,0,1,6,5,4:T(4,128)} %bitcast.659), kind=kLoop, calls=%fused_computation.79 | loop fusion | bytes 147456 | tf_op jit(solution)/shard_map/squeeze | solution.py:120
  114.6 1.2 copy.240
  161.8 164.0 %all-gather.2.cloned.1.call-done = f32[32,2,9216]{2,1,0:T(2,128)} async-done(((f32[1,2,9216]{2,1,0:T(2,128)}), f32[32,2,9216]{2,1,0:T(2,128)}) %all-gather.2.cloned.1.call-update) | async-done | bytes 2359312 | tf_op jit(solution)/shard_map/all_gather | solution.py:212
  326.5 5.6 %scatter_fusion = f32[32,2,9216]{2,1,0:T(2,128)S(1)} fusion(f32[32,2,9216]{2,1,0:T(2,128)S(1)} %broadcast_in_dim.22, s32[32]{0:T(128)S(1)} %fusion.197, f32[32,2,9216]{2,1,0:T(2,128)} %all-gather.2.cloned.1.call-done), kind=kCustom, calls=%fused_computation | custom fusion | bytes 7078016 | tf_op jit(solution)/shard_map/scatter | solution.py:213
  332.1 1.4 copy-done
  (753 shorter events, 104.4 us)
Async XLA Ops:
  6.5 319.3 %all-gather.2.cloned.1.call-start = ((), (), s32[]{:S(2)}) async-start(), calls=%async_computation | async-start | bytes 2433024 | tf_op jit(solution)/shard_map/all_gather | solution.py:212
  76.1 1.9 copy-start.1
  82.9 49.2 %collective-permute-start = (f32[2,2,24,3,128]{4,2,3,1,0:T(8,128)}, f32[2,2,24,3,128]{4,2,3,1,0:T(8,128)}, u32[]{:S(2)}, u32[]{:S(2)}) collective-permute-start(f32[2,2,24,3,128]{4,2,3,1,0:T(8,128)} %copy.195), channel_id=1, source_target_pairs={{0,384},{128,0},{256,128},{384,256},{1,385},{129,1},{257,129},{385... | collective-permute-start | bytes 442376 | tf_op jit(solution)/shard_map/ppermute | solution.py:11
  89.2 52.5 %collective-permute-start.1 = (f32[2,2,24,3,128]{4,2,3,1,0:T(8,128)}, f32[2,2,24,3,128]{4,2,3,1,0:T(8,128)}, u32[]{:S(2)}, u32[]{:S(2)}) collective-permute-start(f32[2,2,24,3,128]{4,2,3,1,0:T(8,128)} %copy.211), channel_id=1, source_target_pairs={{0,112},{16,0},{32,16},{48,32},{64,48},{80,64},{96,80},{112,96},{1... | collective-permute-start | bytes 442376 | tf_op jit(solution)/shard_map/ppermute | solution.py:11
  96.8 6.7 %copy-start.7 = (bf16[4,4,4,2,144]{4,3,2,1,0:T(2,128)(2,1)S(1)}, bf16[4,4,4,2,144]{4,3,2,1,0:T(2,128)(2,1)}, u32[]{:S(2)}) copy-start(bf16[4,4,4,2,144]{4,3,2,1,0:T(2,128)(2,1)} %param.6) | copy-start | bytes 110596
  96.8 54.3 %collective-permute-start.2 = (f32[2,2,24,3,128]{4,2,3,1,0:T(8,128)}, f32[2,2,24,3,128]{4,2,3,1,0:T(8,128)}, u32[]{:S(2)}, u32[]{:S(2)}) collective-permute-start(f32[2,2,24,3,128]{4,2,3,1,0:T(8,128)} %copy.225), channel_id=1, source_target_pairs={{0,15},{1,0},{2,1},{3,2},{4,3},{5,4},{6,5},{7,6},{8,7},{9,8},{10,9... | collective-permute-start | bytes 442376 | tf_op jit(solution)/shard_map/ppermute | solution.py:11
  108.8 5.0 %copy-start.6 = (f32[2,2,24,3,2,4,4,4,1]{2,7,8,6,5,4,3,1,0:T(4,128)S(1)}, f32[2,2,24,3,2,4,4,4,1]{2,7,8,6,5,4,3,1,0:T(4,128)}, u32[]{:S(2)}) copy-start(f32[2,2,24,3,2,4,4,4,1]{2,7,8,6,5,4,3,1,0:T(4,128)} %get-tuple-element.214) | copy-start | bytes 442372
  114.6 1.8 copy-start.5
  117.5 6.8 %copy-start.4 = (f32[2,2,24,3,2,1,4,4,4]{2,7,8,6,5,4,3,1,0:T(4,128)S(1)}, f32[2,2,24,3,2,1,4,4,4]{2,7,8,6,5,4,3,1,0:T(4,128)}, u32[]{:S(2)}) copy-start(f32[2,2,24,3,2,1,4,4,4]{2,7,8,6,5,4,3,1,0:T(4,128)} %get-tuple-element.209) | copy-start | bytes 442372
  124.4 1.2 copy-start.3
  125.8 2.2 copy-start.2
  126.9 3.0 copy-start.8
  127.7 2.8 copy-start.9
  128.0 3.9 %copy-start.10 = (f32[1,3,3,128]{3,0,2,1:T(1,128)S(1)}, f32[1,3,3,128]{3,0,2,1:T(1,128)}, u32[]{:S(2)}) copy-start(f32[1,3,3,128]{3,0,2,1:T(1,128)} %get-tuple-element.293) | copy-start | bytes 13828
  157.9 3.8 %copy-start.11 = (s32[1,32]{1,0:T(1,128)S(1)}, s32[1,32]{1,0:T(1,128)}, u32[]{:S(2)}) copy-start(s32[1,32]{1,0:T(1,128)} %param.7) | copy-start | bytes 388
  332.1 1.4 copy-start
Sparse Core Ops, SparseCore 0:
  161.9 163.8 all-gather.1
where the time goes:
time: 341 us; the launch traced here: 340 us
  waiting for transfers between devices  164 us (48%)
  matrix products  80.8 us (24%)
  local copies, waits for them, and re-layouts  57.4 us (17%)
  between operations  14.1 us (4%)
  other arithmetic  12.7 us (4%)
  starting transfers between devices  9.61 us (3%)
    all_gather x1, waiting for transfers between devices, body(): gathered = lax.all_gather(coarse_block, ('gx', 'gy'), axis=0, tiled=True)  164 us
    ppermute x3, starting transfers between devices, passed_along(): return lax.ppermute(value, axis, pairs)  9.61 us
    dot_general x16, matrix products, inner_block(): jnp.einsum('kr,lr->kl', left_re, right_im, precision=highest)  8.97 us
    dot_general x16, matrix products, inner_block(): jnp.einsum('kr,lr->kl', left_im, right_re, precision=highest)  8.03 us
    slice x7, local copies, waits for them, and re-layouts, boundary_face(): sliced = lax.index_in_dim(basis, layer, 5 + position, keepdims=False)  7.96 us
    dot_general x16, matrix products, inner_block(): jnp.einsum('kr,lr->kl', left_re, right_re, precision=highest)  7.76 us
    dot_general x16, matrix products, inner_block(): jnp.einsum('kr,lr->kl', left_im, right_im, precision=highest)  7.75 us
  transfers between devices with their start and end apart: 4, of which 1 were waited for; matrix products, arithmetic and copies ran while one was open for 17% of the time, Pallas kernels for 0%

commit v1 on v0

v1 whole, which is shorter than its diff:
```python
import jax
import jax.numpy as jnp
import numpy as np
from jax import lax
from jax.experimental import pallas as pl
from jax.experimental.pallas import tpu as pltpu
from jax.sharding import PartitionSpec as P

F32 = jnp.float32
BF16 = jnp.bfloat16
SITES = 64
FACE = 16
NVEC = 24
GROUPS = 12
WIDE = GROUPS * NVEC
PAD = 384
FULL = 4 * WIDE
LINKS = 144
COUNT = 32
TARGET = 64.0
FULL_PRECISION = lax.Precision.HIGHEST
GAMMA = [
    ((0, 1, -1j), (1, 0, -1j)),
    ((0, 1, -1), (1, 0, 1)),
    ((0, 0, -1j), (1, 1, 1j)),
    ((0, 0, 1), (1, 1, 1)),
]


def site_rows(axis, layer):
    rows = []
    for first in range(4):
        for second in range(4):
            place = [first, second]
            place.insert(axis, layer)
            rows.append(place[0] * 16 + place[1] * 4 + place[2])
    return rows


def row_selection():
    sites = []
    for part in range(2):
        sites += [2 * site + part for site in range(SITES)]
    for layer in (3, 0):
        for axis in range(3):
            for part in range(2):
                sites += [2 * site + part for site in site_rows(axis, layer)]
    chosen = np.zeros((len(sites), 2 * SITES), np.float32)
    chosen[np.arange(len(sites)), sites] = 1.0
    return chosen


def gram_fold():
    out = np.zeros((2, WIDE, 128), np.float32)
    for lane in range(WIDE):
        chirality, vector = lane // 144, lane % 24
        for part in range(2):
            out[part, lane, chirality * 48 + part * 24 + vector] = 1.0
    return out


def mixing_spread():
    out = np.zeros((128, 4, PAD), np.float32)
    for part in range(2):
        for chirality in range(2):
            for lane in range(144):
                source = chirality * 48 + part * 24 + lane % 24
                out[source, part * 2 + chirality, chirality * 144 + lane] = 1.0
    return out.reshape(128, 4 * PAD)


def colour_turns():
    out = np.zeros((WIDE, 2, PAD), np.float32)
    for lane in range(WIDE):
        base, colour, vector = lane // 72, lane // 24 % 3, lane % 24
        for turn in (1, 2):
            out[base * 72 + (colour + turn) % 3 * 24 + vector, turn - 1, lane] = 1.0
    return out.reshape(WIDE, 2 * PAD)


def link_spread():
    out = np.zeros((128, 3, PAD), np.float32)
    for lane in range(WIDE):
        colour = lane // 24 % 3
        for turn in range(3):
            out[colour * 3 + (colour + turn) % 3, turn, lane] = 1.0
    return out.reshape(128, 3 * PAD)


def link_pick():
    out = np.zeros((LINKS, 13, 128), np.float32)
    for piece in range(13):
        start = 9 * piece if piece < 12 else 135
        for entry in range(9):
            out[start + entry, piece, entry] = 1.0
    return out.reshape(LINKS, 13 * 128)


def dot(left, right, dims=((1,), (0,)), precision=None):
    return lax.dot_general(left, right, (dims, ((), ())), precision=precision, preferred_element_type=F32)


def time_rows(block):
    return jnp.concatenate([block[:, step * WIDE : (step + 1) * WIDE] for step in range(4)], axis=0)


def lane_of(shape):
    return lax.broadcasted_iota(jnp.int32, shape, 1)


def row_of(shape):
    return lax.broadcasted_iota(jnp.int32, shape, 0)


def mixing_rows(hermitian, hermitian_turned):
    shape = (NVEC, 128)
    lanes, rows = lane_of(shape), row_of(shape)
    lower = lanes < 48
    lower_row = lower[:1]
    mix = jnp.where((lanes % 48 == rows) & (lanes < 96), 1.0, 0.0)
    turned = jnp.where((lanes % 48 == rows + 24) & (lanes < 96), 1.0, 0.0)
    weights = jnp.ones(shape, F32)

    def spread(column, offset):
        first = hermitian[:, offset + column : offset + column + 1]
        second = hermitian[:, 48 + offset + column : 49 + offset + column]
        return jnp.where(lower, first, second)

    for column in range(NVEC):
        row = hermitian[column : column + 1]
        row_turned = hermitian_turned[column : column + 1]
        mix_row = mix[column : column + 1]
        mix_row_turned = turned[column : column + 1]
        product = row * mix_row
        first = jnp.sum(jnp.where(lower_row, product, 0.0), axis=1, keepdims=True)
        second = jnp.sum(jnp.where(lower_row, 0.0, product), axis=1, keepdims=True)
        weight = jnp.where(lower_row, first, second)
        weights = jnp.where(rows == column, weight, weights)
        if column == NVEC - 1:
            break
        ratio = jnp.where(rows > column, TARGET / weight, 0.0)
        by_re = spread(column, 0) * ratio
        by_im = spread(column, 24) * ratio
        hermitian, hermitian_turned = (
            hermitian - (by_re * row + by_im * row_turned),
            hermitian_turned - (by_re * row_turned - by_im * row),
        )
        mix, turned = (
            mix - (by_re * mix_row + by_im * mix_row_turned),
            turned - (by_re * mix_row_turned - by_im * mix_row),
        )
    return mix * jnp.sqrt(TARGET / weights)


def first_kernel(nn_ref, sel_ref, fold_ref, own_ref, start_ref, mix_ref, px_ref, py_ref, pz_ref):
    chosen = dot(sel_ref[...], nn_ref[...]).astype(BF16)
    every = chosen[:128]
    tall = time_rows(every)
    tall_re = time_rows(every[:64])
    tall_im = time_rows(every[64:])
    wide_re = dot(tall, tall, ((0,), (0,)))
    cross = dot(tall_re, tall_im, ((0,), (0,)))
    crossed = dot(tall_im, tall_re, ((0,), (0,)))
    wide_im = cross - crossed
    group = lane_of((NVEC, WIDE)) // NVEC
    fold_re = jnp.zeros((NVEC, WIDE), F32)
    fold_im = jnp.zeros((NVEC, WIDE), F32)
    for index in range(GROUPS):
        here = slice(index * NVEC, (index + 1) * NVEC)
        fold_re = jnp.where(group == index, wide_re[here], fold_re)
        fold_im = jnp.where(group == index, wide_im[here], fold_im)
    to_re = fold_ref[0]
    to_im = fold_ref[1]
    hermitian = dot(fold_re, to_re, precision=FULL_PRECISION) - dot(fold_im, to_im, precision=FULL_PRECISION)
    hermitian_turned = dot(fold_im, to_re, precision=FULL_PRECISION) + dot(fold_re, to_im, precision=FULL_PRECISION)
    mix = mixing_rows(hermitian, hermitian_turned)
    mix_ref[...] = mix
    parts = []
    rest = mix
    for _ in range(3):
        part = rest.astype(BF16).astype(F32)
        parts.append(part)
        rest = rest - part
    nothing = jnp.zeros((8, 128), F32)
    packed = [part[:16] for part in parts] + [jnp.concatenate([part[16:], nothing], axis=0) for part in parts]
    for axis, out in enumerate((px_ref, py_ref, pz_ref)):
        first = 224 + 32 * axis
        out[:32, :] = chosen[first : first + 32]
        for index, piece in enumerate(packed):
            out[32:, index * 128 : (index + 1) * 128] = piece.astype(BF16)
        out[32:, 768:] = jnp.zeros((16, 384), BF16)
    for axis in range(3):
        first = 128 + 32 * axis
        own_ref[axis, :64] = time_rows(chosen[first : first + 16])
        own_ref[axis, 64:] = time_rows(chosen[first + 16 : first + 32])
    own_ref[3] = every[:, 3 * WIDE :]
    start_ref[...] = every[:, :WIDE]


def second_kernel(
    rx_ref, ry_ref, rz_ref, own_ref, start_ref, mix_ref, ga_ref, sel_ref, pick_ref, links_ref, turns_ref, spread_ref,
    code_ref, flat_ref, order_ref,
):
    face_links = dot(sel_ref[:224], ga_ref[...]).astype(BF16)
    picked = dot(face_links, pick_ref[...]).astype(BF16)
    link_rows = []
    for axis in range(3):
        first = 128 + 32 * axis
        for part in range(2):
            for step in range(4):
                piece = axis * 4 + step
                link_rows.append(picked[first + 16 * part : first + 16 * part + 16, piece * 128 : (piece + 1) * 128])
    link_rows.append(picked[:128, 12 * 128 :])
    gauge = dot(jnp.concatenate(link_rows, axis=0), links_ref[...])
    ahead = []
    for ref in (rx_ref, ry_ref, rz_ref):
        ahead.append(time_rows(ref[:16, :]))
        ahead.append(time_rows(ref[16:32, :]))
    ahead.append(start_ref[...])
    ahead = jnp.concatenate(ahead, axis=0)
    turned = dot(ahead, turns_ref[...])
    same = ahead.astype(F32)
    shifted = [same, turned[:, :WIDE], turned[:, PAD : PAD + WIDE]]
    mixings = []
    for ref in (rx_ref, ry_ref, rz_ref):
        total = jnp.zeros((NVEC, 128), F32)
        for index in (2, 1, 0):
            low = ref[32:48, index * 128 : (index + 1) * 128].astype(F32)
            high = ref[32:48, (index + 3) * 128 : (index + 4) * 128].astype(F32)[:8]
            total = total + jnp.concatenate([low, high], axis=0)
        mixings.append(total)
    mixings.append(mix_ref[...])
    spread = dot(jnp.concatenate(mixings, axis=0), spread_ref[...], precision=FULL_PRECISION)
    own_mix = mix_ref[...]
    group = lane_of((NVEC, WIDE)) // NVEC
    halves = []
    for direction in range(4):
        base = direction * 128
        sign = -1.0 if direction == 3 else 1.0
        moved_re = jnp.zeros((64, WIDE), F32)
        moved_im = jnp.zeros((64, WIDE), F32)
        for turn in range(3):
            lanes = slice(turn * PAD, turn * PAD + WIDE)
            u_re = gauge[base : base + 64, lanes]
            u_im = gauge[base + 64 : base + 128, lanes]
            v_re = shifted[turn][base : base + 64]
            v_im = shifted[turn][base + 64 : base + 128]
            moved_re = moved_re + (u_re * v_re - u_im * v_im)
            moved_im = moved_im + (u_re * v_im + u_im * v_re)
        if sign < 0:
            moved_re, moved_im = -moved_re, -moved_im
        top_re = moved_re.astype(BF16)
        top_im = moved_im.astype(BF16)
        low_re = (moved_re - top_re.astype(F32)).astype(BF16)
        low_im = (moved_im - top_im.astype(F32)).astype(BF16)
        mine = own_ref[direction]
        mine = jnp.concatenate([mine, mine], axis=0)
        wide_re = dot(mine, jnp.concatenate([top_re, top_im, low_re, low_im], axis=0), ((0,), (0,)))
        wide_im = dot(mine, jnp.concatenate([top_im, -top_re, low_im, -low_re], axis=0), ((0,), (0,)))
        fold_re, fold_im = [], []
        for chirality in range(2):
            sum_re = jnp.zeros((NVEC, WIDE), F32)
            sum_im = jnp.zeros((NVEC, WIDE), F32)
            for row_spin, col_spin, value in GAMMA[direction]:
                if chirality == 1:
                    row_spin, col_spin, value = col_spin, row_spin, np.conj(value)
                factor = -value
                for colour in range(3):
                    index = chirality * 6 + row_spin * 3 + colour
                    here = slice(index * NVEC, (index + 1) * NVEC)
                    at_re, at_im = wide_re[here], wide_im[here]
                    if np.imag(factor) != 0:
                        over_re, over_im = -float(np.imag(factor)) * at_im, float(np.imag(factor)) * at_re
                    else:
                        over_re, over_im = float(np.real(factor)) * at_re, float(np.real(factor)) * at_im
                    partner = (1 - chirality) * 6 + col_spin * 3 + colour
                    sum_re = jnp.where(group == index, at_re, jnp.where(group == partner, over_re, sum_re))
                    sum_im = jnp.where(group == index, at_im, jnp.where(group == partner, over_im, sum_im))
            fold_re.append(sum_re)
            fold_im.append(sum_im)
        folded = jnp.concatenate(fold_re + fold_im, axis=0)
        rows = slice(direction * NVEC, (direction + 1) * NVEC)
        mix_re = jnp.concatenate([spread[rows, :WIDE], spread[rows, PAD : PAD + WIDE]], axis=0)
        mix_im = jnp.concatenate([spread[rows, 2 * PAD : 2 * PAD + WIDE], spread[rows, 3 * PAD : 3 * PAD + WIDE]], axis=0)
        by_re = dot(folded, mix_re, ((1,), (1,)), FULL_PRECISION)
        by_im = dot(folded, mix_im, ((1,), (1,)), FULL_PRECISION)
        halves.append((by_re[:48] - by_im[48:], by_im[:48] + by_re[48:]))
    square = (NVEC, 48)
    zero = jnp.zeros((NVEC, NVEC), F32)
    left_re = jnp.concatenate(
        [jnp.concatenate([own_mix[:, 0:24], zero], axis=1), jnp.concatenate([zero, own_mix[:, 48:72]], axis=1)], axis=0
    )
    left_im = jnp.concatenate(
        [jnp.concatenate([own_mix[:, 24:48], zero], axis=1), jnp.concatenate([zero, own_mix[:, 72:96]], axis=1)], axis=0
    )
    left = jnp.concatenate([left_re, left_im], axis=0)
    for direction in range(4):
        half_re, half_im = halves[direction]
        on_re = dot(left, half_re, precision=FULL_PRECISION)
        on_im = dot(left, half_im, precision=FULL_PRECISION)
        flat_ref[direction * 96 : direction * 96 + 48, :] = on_re[:48] + on_im[48:]
        flat_ref[direction * 96 + 48 : direction * 96 + 96, :] = on_im[:48] - on_re[48:]
    pieces = [flat_ref[pl.ds(row, 48, stride=8), :] for row in range(8)]
    long = jnp.concatenate(pieces, axis=1)
    for direction in range(4):
        for part in range(2):
            first = (direction * 2 + part) * 6
            for third in range(3):
                target = direction * 36 + third * 2 + part
                order_ref[pl.ds(target, 6, stride=6), :] = long[first : first + 6, third * 128 : (third + 1) * 128]
    powers = []
    for block in range(9):
        values = order_ref[block * 16 : block * 16 + 16, :]
        largest = jnp.max(jnp.abs(values), axis=0, keepdims=True)
        power = jnp.clip(jnp.ceil(jnp.log2(jnp.maximum(largest, 1e-30)) + 1e-3), -100.0, 120.0)
        scaled = values * jnp.exp2(-power) * 32767.0
        scaled = jnp.clip(jnp.round(scaled), -32767.0, 32767.0)
        code_ref[block * 16 : block * 16 + 16, :] = scaled.astype(jnp.int32).astype(jnp.int16)
        powers.append(power)
    powers = jnp.concatenate(powers + [jnp.zeros((7, 128), F32)], axis=0)
    code_ref[144:160, :] = powers.astype(jnp.int32).astype(jnp.int16)


def place_kernel(order, site_ref, code_ref, out_ref):
    for index in range(COUNT):
        target = site_ref[0, order[index]]
        power = code_ref[index, 144:160, :].astype(jnp.int32).astype(F32)
        scale = jnp.exp2(power) * (1.0 / 32767.0)
        for block in range(9):
            values = code_ref[index, block * 16 : block * 16 + 16, :].astype(jnp.int32).astype(F32)
            out_ref[target, block * 16 : block * 16 + 16, :] = values * scale[block : block + 1]


def first_call(block, selection):
    return pl.pallas_call(
        first_kernel,
        out_shape=[
            jax.ShapeDtypeStruct((4, 128, WIDE), BF16),
            jax.ShapeDtypeStruct((128, WIDE), BF16),
            jax.ShapeDtypeStruct((NVEC, 128), F32),
        ]
        + [jax.ShapeDtypeStruct((48, FULL), BF16)] * 3,
        compiler_params=pltpu.CompilerParams(vmem_limit_bytes=40 * 2**20),
        name="gram_and_mixing",
    )(block, selection, jnp.asarray(gram_fold(), F32))


def second_call(faces, own, start, mix, gauge, selection):
    return pl.pallas_call(
        second_kernel,
        out_shape=jax.ShapeDtypeStruct((160, 128), jnp.int16),
        scratch_shapes=[pltpu.VMEM((384, 48), F32), pltpu.VMEM((144, 128), F32)],
        compiler_params=pltpu.CompilerParams(vmem_limit_bytes=40 * 2**20),
        name="coarse_links",
    )(
        *faces, own, start, mix, gauge, selection,
        jnp.asarray(link_pick(), BF16), jnp.asarray(link_spread(), BF16), jnp.asarray(colour_turns(), BF16),
        jnp.asarray(mixing_spread(), F32),
    )


def place_call(site_map, codes, order):
    return pl.pallas_call(
        lambda site_ref, code_ref, out_ref: place_kernel(order, site_ref, code_ref, out_ref),
        in_specs=[pl.BlockSpec(memory_space=pltpu.SMEM), pl.BlockSpec(memory_space=pltpu.VMEM)],
        out_shape=jax.ShapeDtypeStruct((COUNT, 144, 128), F32),
        compiler_params=pltpu.CompilerParams(vmem_limit_bytes=40 * 2**20),
        name="place_links",
    )(site_map, codes)


def passed_back(value, axis):
    count = lax.axis_size(axis)
    return lax.ppermute(value, axis, [(source, (source - 1) % count) for source in range(count)])


def ring_order():
    return [(z % 4) * 8 + (z // 4) * 2 + core for z in range(16) for core in range(2)]


def body(near_null, gauge, site_map):
    selection = jnp.asarray(row_selection(), BF16)
    own, start, mix, *faces = first_call(near_null.reshape(2 * SITES, FULL), selection)
    faces = [passed_back(face, axis) for face, axis in zip(faces, ("gx", "gy", "zt"))]
    code = second_call(faces, own, start, mix, gauge.reshape(2 * SITES, LINKS), selection)
    order = ring_order()
    codes = lax.all_gather(code[None], ("gx", "gy"), axis=0, tiled=True, axis_index_groups=[order])
    placed = place_call(site_map, codes, order)
    placed = placed.reshape(COUNT, 72, 2, 128).transpose(0, 2, 1, 3)
    return placed.reshape(1, COUNT, 2, 9216)


def solution(mesh):
    return jax.shard_map(
        body,
        mesh=mesh,
        in_specs=(P("gx", "gy", "zt", None, None), P("gx", "gy", "zt", None, None), P("zt", None)),
        out_specs=P("zt", None, None, None),
        check_vma=False,
    )
```

time: 341 us -> 77.7 us (0.23)
  the two profiles are of different devices: /device:TPU:39 before, /device:TPU:1 now
where the time goes in v1:
time: 77.7 us; the launch traced here: 77.2 us
  blocking collectives  37.9 us (49%)
  starting transfers between devices  16.8 us (22%)
  Pallas kernels  11.1 us (14%)
  local copies, waits for them, and re-layouts  8.85 us (11%)
  waiting for transfers between devices  2.47 us (3%)
    all_gather x1, blocking collectives, body(): lax.all_gather(code[None], ('gx', 'gy'), axis=0, tiled=True, axis_index_g...  37.9 us
    ppermute x3, starting transfers between devices, passed_back(): lax.ppermute(value, axis, [(source, (source - 1) % count) for source in r...  16.8 us
    unnamed x16, local copies, waits for them, and re-layouts  6.87 us
    pallas_call x1, Pallas kernels, first_call(): pl.pallas_call(first_kernel, out_shape=[jax.ShapeDtypeStruct((4, 128, WID...  4.43 us
    pallas_call x1, Pallas kernels, second_call(): pl.pallas_call(second_kernel, out_shape=jax.ShapeDtypeStruct((160, 128),...  4.37 us
    ppermute x3, waiting for transfers between devices, passed_back(): lax.ppermute(value, axis, [(source, (source - 1) % count) for source in r...  2.47 us
    pallas_call x1, Pallas kernels, place_call(): pl.pallas_call(lambda site_ref, code_ref, out_ref: place_kernel(order, si...  2.25 us
  transfers between devices with their start and end apart: 3, of which 1 were waited for; matrix products, arithmetic and copies ran while one was open for 1% of the time, Pallas kernels for 0%

profile of v1, /device:TPU:1, one launch (start us, length us, event | category | flops | bytes accessed | tf_op | source)
XLA Modules:
  0.0 77.2 jit_solution(5382803357731570857)
XLA Ops:
  0.0 1.1 %reshape.12.nn_ref = bf16[128,1152]{1,0:T(8,128)(2,1)S(1)} reshape(bf16[4,4,4,2,1152]{4,3,2,1,0:T(2,128)(2,1)} %param.9) | data formatting | bytes 589824 | tf_op jit(solution)/shard_map/reshape | solution.py:383
  1.1 0.0 copy-start.3
  1.1 0.9 %copy-done.3 = bf16[320,128]{1,0:T(8,128)(2,1)S(1)} copy-done((bf16[320,128]{1,0:T(8,128)(2,1)S(1)}, bf16[320,128]{1,0:T(8,128)(2,1)}, u32[]{:S(2)}) %copy-start.3) | copy-done | bytes 81944
  2.0 0.0 copy-start.6
  2.0 1.0 %copy-done.6 = f32[2,288,128]{2,1,0:T(8,128)S(1)} copy-done((f32[2,288,128]{2,1,0:T(8,128)S(1)}, f32[2,288,128]{2,1,0:T(8,128)}, u32[]{:S(2)}) %copy-start.6) | copy-done | bytes 294936
  2.9 4.4 %gram_and_mixing.1 = (bf16[4,128,288]{2,1,0:T(8,128)(2,1)S(1)}, bf16[128,288]{1,0:T(8,128)(2,1)S(1)}, f32[24,128]{1,0:T(8,128)S(1)}, bf16[48,1152]{1,0:T(8,128)(...) custom-call(bf16[128,1152]{1,0:T(8,128)(2,1)S(1)} %reshape.12.nn_ref, ...), custom_call_target="tpu_custom_call" | custom-call | tf_op jit(solution)/shard_map/gram_and_mixing/pallas_call | solution.py:335
  7.4 0.0 copy-start.7
  7.4 7.1 %collective-permute-start = (bf16[48,1152]{1,0:T(8,128)(2,1)S(1)}, bf16[48,1152]{1,0:T(8,128)(2,1)S(1)}, u32[]{:S(2)}, u32[]{:S(2)}) collective-permute-start(bf16[48,1152]{1,0:T(8,128)(2,1)S(1)} %get-tuple-element.11), channel_id=1, source_target_pairs={{0,384},{128,0},{256,128},{384,256},{1,385},{129,1},{257,129},{385... | collective-permute-start | bytes 331784 | tf_op jit(solution)/shard_map/ppermute | solution.py:374
  14.5 3.6 %collective-permute-start.1 = (bf16[48,1152]{1,0:T(8,128)(2,1)S(1)}, bf16[48,1152]{1,0:T(8,128)(2,1)S(1)}, u32[]{:S(2)}, u32[]{:S(2)}) collective-permute-start(bf16[48,1152]{1,0:T(8,128)(2,1)S(1)} %get-tuple-element.12), channel_id=1, source_target_pairs={{0,112},{16,0},{32,16},{48,32},{64,48},{80,64},{96,80},{112,96},{1... | collective-permute-start | bytes 331784 | tf_op jit(solution)/shard_map/ppermute | solution.py:374
  18.1 6.1 %collective-permute-start.2 = (bf16[48,1152]{1,0:T(8,128)(2,1)S(1)}, bf16[48,1152]{1,0:T(8,128)(2,1)S(1)}, u32[]{:S(2)}, u32[]{:S(2)}) collective-permute-start(bf16[48,1152]{1,0:T(8,128)(2,1)S(1)} %get-tuple-element.13), channel_id=1, source_target_pairs={{0,15},{1,0},{2,1},{3,2},{4,3},{5,4},{6,5},{7,6},{8,7},{9,8},{10,9... | collective-permute-start | bytes 331784 | tf_op jit(solution)/shard_map/ppermute | solution.py:374
  24.2 0.9 %reshape.13.ga_ref = bf16[128,144]{1,0:T(8,128)(2,1)S(1)} reshape(bf16[4,4,4,2,144]{4,3,2,1,0:T(2,128)(2,1)} %param.10) | data formatting | bytes 73728 | tf_op jit(solution)/shard_map/reshape | solution.py:385
  25.1 0.0 collective-permute-done.rx_ref
  25.1 2.5 %collective-permute-done.1.ry_ref = bf16[48,1152]{1,0:T(8,128)(2,1)S(1)} collective-permute-done((bf16[48,1152]{1,0:T(8,128)(2,1)S(1)}, bf16[48,1152]{1,0:T(8,128)(2,1)S(1)}, u32[]{:S(2)}, u32[]{:S(2)}) %collective-permute-start.1) | collective-permute-done | bytes 110624 | tf_op jit(solution)/shard_map/ppermute | solution.py:374
  27.6 0.0 collective-permute-done.2.rz_ref
  27.6 1.1 %copy-done = f32[128,1536]{1,0:T(8,128)S(1)} copy-done((f32[128,1536]{1,0:T(8,128)S(1)}, f32[128,1536]{1,0:T(8,128)}, u32[]{:S(2)}) %copy-start) | copy-done | bytes 786456
  28.7 0.0 copy-start.1
  28.7 1.0 %copy-done.1 = bf16[144,1664]{1,0:T(8,128)(2,1)S(1)} copy-done((bf16[144,1664]{1,0:T(8,128)(2,1)S(1)}, bf16[144,1664]{1,0:T(8,128)(2,1)}, u32[]{:S(2)}) %copy-start.1) | copy-done | bytes 479256
  29.7 1.0 %copy-done.2 = bf16[288,768]{1,0:T(8,128)(2,1)S(1)} copy-done((bf16[288,768]{1,0:T(8,128)(2,1)S(1)}, bf16[288,768]{1,0:T(8,128)(2,1)}, u32[]{:S(2)}) %copy-start.2) | copy-done | bytes 442392
  30.8 0.9 %copy-done.4 = bf16[320,128]{1,0:T(8,128)(2,1)S(1)} copy-done((bf16[320,128]{1,0:T(8,128)(2,1)S(1)}, bf16[320,128]{1,0:T(8,128)(2,1)}, u32[]{:S(2)}) %copy-start.4) | copy-done | bytes 81944
  31.6 1.0 %copy-done.5 = bf16[128,1152]{1,0:T(8,128)(2,1)S(1)} copy-done((bf16[128,1152]{1,0:T(8,128)(2,1)S(1)}, bf16[128,1152]{1,0:T(8,128)(2,1)}, u32[]{:S(2)}) %copy-start.5) | copy-done | bytes 294936
  32.6 4.4 %coarse_links.1 = s16[160,128]{1,0:T(8,128)(2,1)S(1)} custom-call(bf16[48,1152]{1,0:T(8,128)(2,1)S(1)} %collective-permute-done.rx_ref, bf16[48,1152]{1,0:T(8,128)(2,1)S(1)} %collective-permute-done.1.ry_ref, bf16[48,1152]{1,0:T(8,128)(2,1)S(1)} %collective-permute-done.2.rz_ref, bf16[4,128,288]{2,1,0:T(8,128)(2,1)S(1)} %get-tuple-element.14.own_ref, ...), custom_call_target="tpu_custom_call" | custom-call | tf_op jit(solution)/shard_map/coarse_links/pallas_call | solution.py:349
  37.0 37.9 %all-gather.2 = s16[5120,128]{1,0:T(8,128)(2,1)S(1)} all-gather(s16[160,128]{1,0:T(8,128)(2,1)S(1)} %coarse_links.1), channel_id=2, replica_groups={{0,16,128,144,256,272,384,400,32,48,160,176,288,304,416,432,64,80,192,2..., dimensions={0}, use_global_device_ids=true | all-gather | bytes 1351680 | tf_op jit(solution)/shard_map/all_gather | solution.py:387
  74.9 0.0 copy-done.7
  74.9 2.3 %place_links.1 = f32[32,144,128]{2,1,0:T(8,128)} custom-call(s32[1,32]{1,0:T(1,128)S(1)} %copy-done.7, s16[32,160,128]{2,1,0:T(8,128)(2,1)S(1)} %bitcast.6), custom_call_target="tpu_custom_call" | custom-call | tf_op jit(solution)/shard_map/place_links/pallas_call | solution.py:363
  (4 shorter events, 0.0 us)
Async XLA Ops:
  1.1 0.9 %copy-start.3 = (bf16[320,128]{1,0:T(8,128)(2,1)S(1)}, bf16[320,128]{1,0:T(8,128)(2,1)}, u32[]{:S(2)}) copy-start(bf16[320,128]{1,0:T(8,128)(2,1)} %constant.12.clone.sel_ref) | copy-start | bytes 245764
  2.0 1.0 %copy-start.6 = (f32[2,288,128]{2,1,0:T(8,128)S(1)}, f32[2,288,128]{2,1,0:T(8,128)}, u32[]{:S(2)}) copy-start(f32[2,288,128]{2,1,0:T(8,128)} %constant.13.clone.fold_ref) | copy-start | bytes 884740
  7.4 67.6 %copy-start.7 = (s32[1,32]{1,0:T(1,128)S(1)}, s32[1,32]{1,0:T(1,128)}, u32[]{:S(2)}) copy-start(s32[1,32]{1,0:T(1,128)} %site_ref.1) | copy-start | bytes 388
  7.4 17.7 %collective-permute-start = (bf16[48,1152]{1,0:T(8,128)(2,1)S(1)}, bf16[48,1152]{1,0:T(8,128)(2,1)S(1)}, u32[]{:S(2)}, u32[]{:S(2)}) collective-permute-start(bf16[48,1152]{1,0:T(8,128)(2,1)S(1)} %get-tuple-element.11), channel_id=1, source_target_pairs={{0,384},{128,0},{256,128},{384,256},{1,385},{129,1},{257,129},{385... | collective-permute-start | bytes 331784 | tf_op jit(solution)/shard_map/ppermute | solution.py:374
  14.5 13.1 %collective-permute-start.1 = (bf16[48,1152]{1,0:T(8,128)(2,1)S(1)}, bf16[48,1152]{1,0:T(8,128)(2,1)S(1)}, u32[]{:S(2)}, u32[]{:S(2)}) collective-permute-start(bf16[48,1152]{1,0:T(8,128)(2,1)S(1)} %get-tuple-element.12), channel_id=1, source_target_pairs={{0,112},{16,0},{32,16},{48,32},{64,48},{80,64},{96,80},{112,96},{1... | collective-permute-start | bytes 331784 | tf_op jit(solution)/shard_map/ppermute | solution.py:374
  18.1 9.5 %collective-permute-start.2 = (bf16[48,1152]{1,0:T(8,128)(2,1)S(1)}, bf16[48,1152]{1,0:T(8,128)(2,1)S(1)}, u32[]{:S(2)}, u32[]{:S(2)}) collective-permute-start(bf16[48,1152]{1,0:T(8,128)(2,1)S(1)} %get-tuple-element.13), channel_id=1, source_target_pairs={{0,15},{1,0},{2,1},{3,2},{4,3},{5,4},{6,5},{7,6},{8,7},{9,8},{10,9... | collective-permute-start | bytes 331784 | tf_op jit(solution)/shard_map/ppermute | solution.py:374
  27.6 1.1 %copy-start = (f32[128,1536]{1,0:T(8,128)S(1)}, f32[128,1536]{1,0:T(8,128)}, u32[]{:S(2)}) copy-start(f32[128,1536]{1,0:T(8,128)} %constant.17.clone.spread_ref) | copy-start | bytes 2359300
  28.7 1.0 %copy-start.1 = (bf16[144,1664]{1,0:T(8,128)(2,1)S(1)}, bf16[144,1664]{1,0:T(8,128)(2,1)}, u32[]{:S(2)}) copy-start(bf16[144,1664]{1,0:T(8,128)(2,1)} %constant.14.clone.pick_ref) | copy-start | bytes 1437700
  29.7 1.0 %copy-start.2 = (bf16[288,768]{1,0:T(8,128)(2,1)S(1)}, bf16[288,768]{1,0:T(8,128)(2,1)}, u32[]{:S(2)}) copy-start(bf16[288,768]{1,0:T(8,128)(2,1)} %constant.16.clone.turns_ref) | copy-start | bytes 1327108
  30.8 0.9 %copy-start.4 = (bf16[320,128]{1,0:T(8,128)(2,1)S(1)}, bf16[320,128]{1,0:T(8,128)(2,1)}, u32[]{:S(2)}) copy-start(bf16[320,128]{1,0:T(8,128)(2,1)} %constant.12.clone.sel_ref) | copy-start | bytes 245764
  31.6 1.0 %copy-start.5 = (bf16[128,1152]{1,0:T(8,128)(2,1)S(1)}, bf16[128,1152]{1,0:T(8,128)(2,1)}, u32[]{:S(2)}) copy-start(bf16[128,1152]{1,0:T(8,128)(2,1)} %constant.15.clone.links_ref) | copy-start | bytes 884740

commit v2 on v1

--- a/solution.py
+++ b/solution.py
@@ -17,6 +17,8 @@
 FULL = 4 * WIDE
 LINKS = 144
 COUNT = 32
+MIX_ROW = 288
+SENT = 368
 TARGET = 64.0
 FULL_PRECISION = lax.Precision.HIGHEST
 GAMMA = [
@@ -27,89 +29,86 @@
 ]
 
 
-def site_rows(axis, layer):
-    rows = []
-    for first in range(4):
-        for second in range(4):
-            place = [first, second]
-            place.insert(axis, layer)
-            rows.append(place[0] * 16 + place[1] * 4 + place[2])
-    return rows
-
-
-def row_selection():
-    sites = []
-    for part in range(2):
-        sites += [2 * site + part for site in range(SITES)]
-    for layer in (3, 0):
-        for axis in range(3):
-            for part in range(2):
-                sites += [2 * site + part for site in site_rows(axis, layer)]
-    chosen = np.zeros((len(sites), 2 * SITES), np.float32)
-    chosen[np.arange(len(sites)), sites] = 1.0
-    return chosen
+def dot(left, right, dims=((1,), (0,)), precision=None):
+    return lax.dot_general(left, right, (dims, ((), ())), precision=precision, preferred_element_type=F32)
+
+
+def time_rows(block):
+    return jnp.concatenate([block[:, step * WIDE : (step + 1) * WIDE] for step in range(4)], axis=0)
+
+
+def lane_of(shape):
+    return lax.broadcasted_iota(jnp.int32, shape, 1)
+
+
+def row_of(shape):
+    return lax.broadcasted_iota(jnp.int32, shape, 0)
+
+
+def ones_where(condition, dtype):
+    return jnp.where(condition, 1.0, 0.0).astype(dtype)
+
+
+def all_rows():
+    shape = (SITES, 2 * SITES)
+    first = lane_of(shape) - 2 * row_of(shape)
+    return [ones_where(first == part, BF16) for part in range(2)]
+
+
+def layer_rows(layer):
+    shape = (FACE, 2 * SITES)
+    lanes, rows = lane_of(shape), row_of(shape)
+    sites = [layer * 16 + rows, (rows // 4) * 16 + layer * 4 + rows % 4, rows * 4 + layer]
+    return [ones_where(lanes == 2 * site + part, BF16) for site in sites for part in range(2)]
 
 
 def gram_fold():
-    out = np.zeros((2, WIDE, 128), np.float32)
-    for lane in range(WIDE):
-        chirality, vector = lane // 144, lane % 24
-        for part in range(2):
-            out[part, lane, chirality * 48 + part * 24 + vector] = 1.0
-    return out
+    shape = (WIDE, 128)
+    rows = row_of(shape)
+    away = lane_of(shape) - ((rows // 144) * 48 + rows % NVEC)
+    return jnp.concatenate([ones_where(away == part * NVEC, F32) for part in range(2)], axis=1)
 
 
 def mixing_spread():
-    out = np.zeros((128, 4, PAD), np.float32)
+    shape = (128, PAD)
+    lanes, rows = lane_of(shape), row_of(shape)
+    blocks = []
     for part in range(2):
         for chirality in range(2):
-            for lane in range(144):
-                source = chirality * 48 + part * 24 + lane % 24
-                out[source, part * 2 + chirality, chirality * 144 + lane] = 1.0
-    return out.reshape(128, 4 * PAD)
+            inside = (lanes >= chirality * 144) & (lanes < chirality * 144 + 144)
+            source = jnp.where(inside, lanes % NVEC + chirality * 48 + part * NVEC, -1)
+            blocks.append(ones_where(rows == source, F32))
+    return jnp.concatenate(blocks, axis=1)
 
 
 def colour_turns():
-    out = np.zeros((WIDE, 2, PAD), np.float32)
-    for lane in range(WIDE):
-        base, colour, vector = lane // 72, lane // 24 % 3, lane % 24
-        for turn in (1, 2):
-            out[base * 72 + (colour + turn) % 3 * 24 + vector, turn - 1, lane] = 1.0
-    return out.reshape(WIDE, 2 * PAD)
+    shape = (WIDE, PAD)
+    lanes, rows = lane_of(shape), row_of(shape)
+    colour = (lanes // NVEC) % 3
+    blocks = []
+    for turn in (1, 2):
+        source = lanes + NVEC * jnp.where(colour + turn >= 3, turn - 3, turn)
+        blocks.append(ones_where((rows == source) & (lanes < WIDE), BF16))
+    return jnp.concatenate(blocks, axis=1)
 
 
 def link_spread():
-    out = np.zeros((128, 3, PAD), np.float32)
-    for lane in range(WIDE):
-        colour = lane // 24 % 3
-        for turn in range(3):
-            out[colour * 3 + (colour + turn) % 3, turn, lane] = 1.0
-    return out.reshape(128, 3 * PAD)
+    shape = (16, PAD)
+    lanes, rows = lane_of(shape), row_of(shape)
+    colour = (lanes // NVEC) % 3
+    blocks = []
+    for turn in range(3):
+        source = colour * 3 + (colour + turn) % 3
+        blocks.append(ones_where((rows == source) & (lanes < WIDE), BF16))
+    return jnp.concatenate(blocks, axis=1)
 
 
 def link_pick():
-    out = np.zeros((LINKS, 13, 128), np.float32)
-    for piece in range(13):
-        start = 9 * piece if piece < 12 else 135
-        for entry in range(9):
-            out[start + entry, piece, entry] = 1.0
-    return out.reshape(LINKS, 13 * 128)
-
-
-def dot(left, right, dims=((1,), (0,)), precision=None):
-    return lax.dot_general(left, right, (dims, ((), ())), precision=precision, preferred_element_type=F32)
-
-
-def time_rows(block):
-    return jnp.concatenate([block[:, step * WIDE : (step + 1) * WIDE] for step in range(4)], axis=0)
-
-
-def lane_of(shape):
-    return lax.broadcasted_iota(jnp.int32, shape, 1)
-
-
-def row_of(shape):
-    return lax.broadcasted_iota(jnp.int32, shape, 0)
+    shape = (LINKS, 128)
+    lanes = lane_of(shape)
+    start = jnp.where(lanes < 9, row_of(shape) - lanes, -1)
+    starts = [9 * piece for piece in range(12)] + [135]
+    return jnp.concatenate([ones_where(start == first, BF16) for first in starts], axis=1)
 
 
 def mixing_rows(hermitian, hermitian_turned):
@@ -152,16 +151,14 @@
     return mix * jnp.sqrt(TARGET / weights)
 
 
-def first_kernel(nn_ref, sel_ref, fold_ref, own_ref, start_ref, mix_ref, px_ref, py_ref, pz_ref):
-    chosen = dot(sel_ref[...], nn_ref[...]).astype(BF16)
+def first_kernel(nn_ref, own_ref, start_ref, mix_ref, py_ref, px_ref, pz_ref):
+    selection = jnp.concatenate(all_rows() + layer_rows(3) + layer_rows(0), axis=0)
+    chosen = dot(selection, nn_ref[...]).astype(BF16)
     every = chosen[:128]
     tall = time_rows(every)
-    tall_re = time_rows(every[:64])
-    tall_im = time_rows(every[64:])
+    tall_turned = time_rows(jnp.concatenate([every[64:], -every[:64]], axis=0))
     wide_re = dot(tall, tall, ((0,), (0,)))
-    cross = dot(tall_re, tall_im, ((0,), (0,)))
-    crossed = dot(tall_im, tall_re, ((0,), (0,)))
-    wide_im = cross - crossed
+    wide_im = dot(tall, tall_turned, ((0,), (0,)))
     group = lane_of((NVEC, WIDE)) // NVEC
     fold_re = jnp.zeros((NVEC, WIDE), F32)
     fold_im = jnp.zeros((NVEC, WIDE), F32)
@@ -169,10 +166,9 @@
         here = slice(index * NVEC, (index + 1) * NVEC)
         fold_re = jnp.where(group == index, wide_re[here], fold_re)
         fold_im = jnp.where(group == index, wide_im[here], fold_im)
-    to_re = fold_ref[0]
-    to_im = fold_ref[1]
-    hermitian = dot(fold_re, to_re, precision=FULL_PRECISION) - dot(fold_im, to_im, precision=FULL_PRECISION)
-    hermitian_turned = dot(fold_im, to_re, precision=FULL_PRECISION) + dot(fold_re, to_im, precision=FULL_PRECISION)
+    folded = dot(jnp.concatenate([fold_re, fold_im], axis=0), gram_fold(), precision=FULL_PRECISION)
+    hermitian = folded[:NVEC, :128] - folded[NVEC:, 128:]
+    hermitian_turned = folded[NVEC:, :128] + folded[:NVEC, 128:]
     mix = mixing_rows(hermitian, hermitian_turned)
     mix_ref[...] = mix
     parts = []
@@ -181,14 +177,12 @@
         part = rest.astype(BF16).astype(F32)
         parts.append(part)
         rest = rest - part
-    nothing = jnp.zeros((8, 128), F32)
-    packed = [part[:16] for part in parts] + [jnp.concatenate([part[16:], nothing], axis=0) for part in parts]
+    packed = jnp.concatenate(parts + [jnp.zeros((8, 128), F32)], axis=0).astype(BF16)
     for axis, out in enumerate((px_ref, py_ref, pz_ref)):
         first = 224 + 32 * axis
-        out[:32, :] = chosen[first : first + 32]
-        for index, piece in enumerate(packed):
-            out[32:, index * 128 : (index + 1) * 128] = piece.astype(BF16)
-        out[32:, 768:] = jnp.zeros((16, 384), BF16)
+        for column in range(9):
+            out[column * 32 : column * 32 + 32, :] = chosen[first : first + 32, column * 128 : (column + 1) * 128]
+        out[MIX_ROW:, :] = packed
     for axis in range(3):
         first = 128 + 32 * axis
         own_ref[axis, :64] = time_rows(chosen[first : first + 16])
@@ -198,39 +192,36 @@
 
 
 def second_kernel(
-    rx_ref, ry_ref, rz_ref, own_ref, start_ref, mix_ref, ga_ref, sel_ref, pick_ref, links_ref, turns_ref, spread_ref,
-    code_ref, flat_ref, order_ref,
+    rx_ref, ry_ref, rz_ref, own_ref, start_ref, mix_ref, ga_ref, code_ref, flat_ref, order_ref
 ):
-    face_links = dot(sel_ref[:224], ga_ref[...]).astype(BF16)
-    picked = dot(face_links, pick_ref[...]).astype(BF16)
+    selection = jnp.concatenate(all_rows() + layer_rows(3), axis=0)
+    face_links = dot(selection, ga_ref[...]).astype(BF16)
+    picked = dot(face_links, link_pick()).astype(BF16)
     link_rows = []
     for axis in range(3):
         first = 128 + 32 * axis
         for part in range(2):
             for step in range(4):
                 piece = axis * 4 + step
-                link_rows.append(picked[first + 16 * part : first + 16 * part + 16, piece * 128 : (piece + 1) * 128])
-    link_rows.append(picked[:128, 12 * 128 :])
-    gauge = dot(jnp.concatenate(link_rows, axis=0), links_ref[...])
+                link_rows.append(picked[first + 16 * part : first + 16 * part + 16, piece * 128 : piece * 128 + 16])
+    link_rows.append(picked[:128, 12 * 128 : 12 * 128 + 16])
+    gauge = dot(jnp.concatenate(link_rows, axis=0), link_spread())
     ahead = []
     for ref in (rx_ref, ry_ref, rz_ref):
-        ahead.append(time_rows(ref[:16, :]))
-        ahead.append(time_rows(ref[16:32, :]))
+        face = jnp.concatenate([ref[column * 32 : column * 32 + 32, :] for column in range(9)], axis=1)
+        ahead.append(time_rows(face[:16]))
+        ahead.append(time_rows(face[16:]))
     ahead.append(start_ref[...])
     ahead = jnp.concatenate(ahead, axis=0)
-    turned = dot(ahead, turns_ref[...])
+    turned = dot(ahead, colour_turns())
     same = ahead.astype(F32)
     shifted = [same, turned[:, :WIDE], turned[:, PAD : PAD + WIDE]]
     mixings = []
     for ref in (rx_ref, ry_ref, rz_ref):
-        total = jnp.zeros((NVEC, 128), F32)
-        for index in (2, 1, 0):
-            low = ref[32:48, index * 128 : (index + 1) * 128].astype(F32)
-            high = ref[32:48, (index + 3) * 128 : (index + 4) * 128].astype(F32)[:8]
-            total = total + jnp.concatenate([low, high], axis=0)
-        mixings.append(total)
+        parts = ref[MIX_ROW:SENT, :].astype(F32)
+        mixings.append(parts[48:72] + parts[24:48] + parts[:24])
     mixings.append(mix_ref[...])
-    spread = dot(jnp.concatenate(mixings, axis=0), spread_ref[...], precision=FULL_PRECISION)
+    spread = dot(jnp.concatenate(mixings, axis=0), mixing_spread(), precision=FULL_PRECISION)
     own_mix = mix_ref[...]
     group = lane_of((NVEC, WIDE)) // NVEC
     halves = []
@@ -331,7 +322,7 @@
             out_ref[target, block * 16 : block * 16 + 16, :] = values * scale[block : block + 1]
 
 
-def first_call(block, selection):
+def first_call(block):
     return pl.pallas_call(
         first_kernel,
         out_shape=[
@@ -339,24 +330,20 @@
             jax.ShapeDtypeStruct((128, WIDE), BF16),
             jax.ShapeDtypeStruct((NVEC, 128), F32),
         ]
-        + [jax.ShapeDtypeStruct((48, FULL), BF16)] * 3,
+        + [jax.ShapeDtypeStruct((SENT, 128), BF16)] * 3,
         compiler_params=pltpu.CompilerParams(vmem_limit_bytes=40 * 2**20),
         name="gram_and_mixing",
-    )(block, selection, jnp.asarray(gram_fold(), F32))
-
-
-def second_call(faces, own, start, mix, gauge, selection):
+    )(block)
+
+
+def second_call(faces, own, start, mix, gauge):
     return pl.pallas_call(
         second_kernel,
         out_shape=jax.ShapeDtypeStruct((160, 128), jnp.int16),
         scratch_shapes=[pltpu.VMEM((384, 48), F32), pltpu.VMEM((144, 128), F32)],
         compiler_params=pltpu.CompilerParams(vmem_limit_bytes=40 * 2**20),
         name="coarse_links",
-    )(
-        *faces, own, start, mix, gauge, selection,
-        jnp.asarray(link_pick(), BF16), jnp.asarray(link_spread(), BF16), jnp.asarray(colour_turns(), BF16),
-        jnp.asarray(mixing_spread(), F32),
-    )
+    )(*faces, own, start, mix, gauge)
 
 
 def place_call(site_map, codes, order):
@@ -374,17 +361,26 @@
     return lax.ppermute(value, axis, [(source, (source - 1) % count) for source in range(count)])
 
 
-def ring_order():
-    return [(z % 4) * 8 + (z // 4) * 2 + core for z in range(16) for core in range(2)]
+def flat_index(z, core):
+    return (z % 4) * 8 + (z // 4) * 2 + core
+
+
+def gathered(code):
+    pairs = [[flat_index(z, core), flat_index(z + 1, core)] for z in range(0, 16, 2) for core in range(2)]
+    rings = [[flat_index(z + odd, core) for z in range(0, 16, 2) for core in range(2)] for odd in range(2)]
+    names = ("gx", "gy")
+    code = lax.all_gather(code[None], names, axis=0, tiled=True, axis_index_groups=pairs)
+    code = lax.all_gather(code, names, axis=0, tiled=True, axis_index_groups=rings)
+    return code, [index for pair in pairs for index in pair]
 
 
 def body(near_null, gauge, site_map):
-    selection = jnp.asarray(row_selection(), BF16)
-    own, start, mix, *faces = first_call(near_null.reshape(2 * SITES, FULL), selection)
-    faces = [passed_back(face, axis) for face, axis in zip(faces, ("gx", "gy", "zt"))]
-    code = second_call(faces, own, start, mix, gauge.reshape(2 * SITES, LINKS), selection)
-    order = ring_order()
-    codes = lax.all_gather(code[None], ("gx", "gy"), axis=0, tiled=True, axis_index_groups=[order])
+    own, start, mix, face_y, face_x, face_z = first_call(near_null.reshape(2 * SITES, FULL))
+    face_y = passed_back(face_y, "gy")
+    face_x = passed_back(face_x, "gx")
+    face_z = passed_back(face_z, "zt")
+    code = second_call((face_x, face_y, face_z), own, start, mix, gauge.reshape(2 * SITES, LINKS))
+    codes, order = gathered(code)
     placed = place_call(site_map, codes, order)
     placed = placed.reshape(COUNT, 72, 2, 128).transpose(0, 2, 1, 3)
     return placed.reshape(1, COUNT, 2, 9216)

time: 77.7 us -> 69.7 us (0.90)
  local copies, waits for them, and re-layouts: 8.85 us -> 1.99 us
    unnamed x16 -> x2, local copies, waits for them, and re-layouts: 6.87 us -> 0.01 us
    all_gather x1 -> x2, blocking collectives: 37.9 us -> 37.3 us  [the longest x1 33.8 us: gathered(): lax.all_gather(code, names, axis=0, tiled=True, axis_index_groups=rings)]
where the time goes in v2:
time: 69.7 us; the launch traced here: 69.4 us
  blocking collectives  37.3 us (54%)
  starting transfers between devices  16.8 us (24%)
  Pallas kernels  11.2 us (16%)
  waiting for transfers between devices  2.09 us (3%)
  local copies, waits for them, and re-layouts  1.99 us (3%)
    all_gather x1, blocking collectives, gathered(): lax.all_gather(code, names, axis=0, tiled=True, axis_index_groups=rings)  33.8 us
    ppermute x3, starting transfers between devices, passed_back(): lax.ppermute(value, axis, [(source, (source - 1) % count) for source in r...  16.8 us
    pallas_call x1, Pallas kernels, second_call(): pl.pallas_call(second_kernel, out_shape=jax.ShapeDtypeStruct((160, 128),...  4.45 us
    pallas_call x1, Pallas kernels, first_call(): pl.pallas_call(first_kernel, out_shape=[jax.ShapeDtypeStruct((4, 128, WID...  4.45 us
    all_gather x1, blocking collectives, gathered(): lax.all_gather(code[None], names, axis=0, tiled=True, axis_index_groups=p...  3.53 us
    pallas_call x1, Pallas kernels, place_call(): pl.pallas_call(lambda site_ref, code_ref, out_ref: place_kernel(order, si...  2.25 us
    ppermute x3, waiting for transfers between devices, passed_back(): lax.ppermute(value, axis, [(source, (source - 1) % count) for source in r...  2.09 us
  transfers between devices with their start and end apart: 3, of which 1 were waited for; matrix products, arithmetic and copies ran while one was open for 1% of the time, Pallas kernels for 0%

profile of v2, /device:TPU:1, one launch (start us, length us, event | category | flops | bytes accessed | tf_op | source)
XLA Modules:
  0.0 69.4 jit_solution(11355070371048388831)
XLA Ops:
  0.0 0.0 copy-start
  0.0 1.1 %reshape.12.nn_ref = bf16[128,1152]{1,0:T(8,128)(2,1)S(1)} reshape(bf16[4,4,4,2,1152]{4,3,2,1,0:T(2,128)(2,1)} %param.3) | data formatting | bytes 589824 | tf_op jit(solution)/shard_map/reshape | solution.py:378
  1.1 4.4 %gram_and_mixing.1 = (bf16[4,128,288]{2,1,0:T(8,128)(2,1)S(1)}, bf16[128,288]{1,0:T(8,128)(2,1)S(1)}, f32[24,128]{1,0:T(8,128)S(1)}, bf16[368,128]{1,0:T(8,128)(...) custom-call(bf16[128,1152]{1,0:T(8,128)(2,1)S(1)} %reshape.12.nn_ref), custom_call_target="tpu_custom_call" | custom-call | tf_op jit(solution)/shard_map/gram_and_mixing/pallas_call | solution.py:326
  5.5 7.1 %collective-permute-start = (bf16[368,128]{1,0:T(8,128)(2,1)S(1)}, bf16[368,128]{1,0:T(8,128)(2,1)S(1)}, u32[]{:S(2)}, u32[]{:S(2)}) collective-permute-start(bf16[368,128]{1,0:T(8,128)(2,1)S(1)} %get-tuple-element.11), channel_id=1, source_target_pairs={{0,384},{128,0},{256,128},{384,256},{1,385},{129,1},{257,129},{385... | collective-permute-start | bytes 282632 | tf_op jit(solution)/shard_map/ppermute | solution.py:361
  12.6 3.6 %collective-permute-start.1 = (bf16[368,128]{1,0:T(8,128)(2,1)S(1)}, bf16[368,128]{1,0:T(8,128)(2,1)S(1)}, u32[]{:S(2)}, u32[]{:S(2)}) collective-permute-start(bf16[368,128]{1,0:T(8,128)(2,1)S(1)} %get-tuple-element.12), channel_id=1, source_target_pairs={{0,112},{16,0},{32,16},{48,32},{64,48},{80,64},{96,80},{112,96},{1... | collective-permute-start | bytes 282632 | tf_op jit(solution)/shard_map/ppermute | solution.py:361
  16.3 6.1 %collective-permute-start.2 = (bf16[368,128]{1,0:T(8,128)(2,1)S(1)}, bf16[368,128]{1,0:T(8,128)(2,1)S(1)}, u32[]{:S(2)}, u32[]{:S(2)}) collective-permute-start(bf16[368,128]{1,0:T(8,128)(2,1)S(1)} %get-tuple-element.13), channel_id=1, source_target_pairs={{0,15},{1,0},{2,1},{3,2},{4,3},{5,4},{6,5},{7,6},{8,7},{9,8},{10,9... | collective-permute-start | bytes 282632 | tf_op jit(solution)/shard_map/ppermute | solution.py:361
  22.4 0.9 %reshape.13.ga_ref = bf16[128,144]{1,0:T(8,128)(2,1)S(1)} reshape(bf16[4,4,4,2,144]{4,3,2,1,0:T(2,128)(2,1)} %param.4) | data formatting | bytes 73728 | tf_op jit(solution)/shard_map/reshape | solution.py:382
  23.3 0.0 collective-permute-done.rx_ref
  23.3 2.1 %collective-permute-done.1.ry_ref = bf16[368,128]{1,0:T(8,128)(2,1)S(1)} collective-permute-done((bf16[368,128]{1,0:T(8,128)(2,1)S(1)}, bf16[368,128]{1,0:T(8,128)(2,1)S(1)}, u32[]{:S(2)}, u32[]{:S(2)}) %collective-permute-start.1) | collective-permute-done | bytes 94240 | tf_op jit(solution)/shard_map/ppermute | solution.py:361
  25.4 0.0 collective-permute-done.2.rz_ref
  25.4 4.5 %coarse_links.1 = s16[160,128]{1,0:T(8,128)(2,1)S(1)} custom-call(bf16[368,128]{1,0:T(8,128)(2,1)S(1)} %collective-permute-done.rx_ref, bf16[368,128]{1,0:T(8,128)(2,1)S(1)} %collective-permute-done.1.ry_ref, bf16[368,128]{1,0:T(8,128)(2,1)S(1)} %collective-permute-done.2.rz_ref, bf16[4,128,288]{2,1,0:T(8,128)(2,1)S(1)} %get-tuple-element.14.own_ref, ...), custom_call_target="tpu_custom_call" | custom-call | tf_op jit(solution)/shard_map/coarse_links/pallas_call | solution.py:340
  29.8 3.5 %all-gather = s16[320,128]{1,0:T(8,128)(2,1)S(1)} all-gather(s16[160,128]{1,0:T(8,128)(2,1)S(1)} %coarse_links.1), channel_id=2, replica_groups={{0,128},{16,144},{256,384},{272,400},{32,160},{48,176},{288,416},{304,4..., dimensions={0}, use_global_device_ids=true | all-gather | bytes 122880 | tf_op jit(solution)/shard_map/all_gather | solution.py:372
  33.3 33.8 %all-gather.2.code_ref = s16[32,160,128]{2,1,0:T(8,128)(2,1)S(1)} all-gather(s16[2,160,128]{2,1,0:T(8,128)(2,1)S(1)} %bitcast.6), channel_id=1, replica_groups={{0,16,256,272,32,48,288,304,64,80,320,336,96,112,352,368},{128,144,384,..., dimensions={0}, use_global_device_ids=true | all-gather | bytes 1392640 | tf_op jit(solution)/shard_map/all_gather | solution.py:373
  67.2 0.0 copy-done
  67.2 2.3 %place_links.1 = f32[32,144,128]{2,1,0:T(8,128)} custom-call(s32[1,32]{1,0:T(1,128)S(1)} %copy-done, s16[32,160,128]{2,1,0:T(8,128)(2,1)S(1)} %all-gather.2.code_ref), custom_call_target="tpu_custom_call" | custom-call | tf_op jit(solution)/shard_map/place_links/pallas_call | solution.py:350
Async XLA Ops:
  0.0 67.2 %copy-start = (s32[1,32]{1,0:T(1,128)S(1)}, s32[1,32]{1,0:T(1,128)}, u32[]{:S(2)}) copy-start(s32[1,32]{1,0:T(1,128)} %site_ref.1) | copy-start | bytes 388
  5.5 17.7 %collective-permute-start = (bf16[368,128]{1,0:T(8,128)(2,1)S(1)}, bf16[368,128]{1,0:T(8,128)(2,1)S(1)}, u32[]{:S(2)}, u32[]{:S(2)}) collective-permute-start(bf16[368,128]{1,0:T(8,128)(2,1)S(1)} %get-tuple-element.11), channel_id=1, source_target_pairs={{0,384},{128,0},{256,128},{384,256},{1,385},{129,1},{257,129},{385... | collective-permute-start | bytes 282632 | tf_op jit(solution)/shard_map/ppermute | solution.py:361
  12.6 12.7 %collective-permute-start.1 = (bf16[368,128]{1,0:T(8,128)(2,1)S(1)}, bf16[368,128]{1,0:T(8,128)(2,1)S(1)}, u32[]{:S(2)}, u32[]{:S(2)}) collective-permute-start(bf16[368,128]{1,0:T(8,128)(2,1)S(1)} %get-tuple-element.12), channel_id=1, source_target_pairs={{0,112},{16,0},{32,16},{48,32},{64,48},{80,64},{96,80},{112,96},{1... | collective-permute-start | bytes 282632 | tf_op jit(solution)/shard_map/ppermute | solution.py:361
  16.3 9.1 %collective-permute-start.2 = (bf16[368,128]{1,0:T(8,128)(2,1)S(1)}, bf16[368,128]{1,0:T(8,128)(2,1)S(1)}, u32[]{:S(2)}, u32[]{:S(2)}) collective-permute-start(bf16[368,128]{1,0:T(8,128)(2,1)S(1)} %get-tuple-element.13), channel_id=1, source_target_pairs={{0,15},{1,0},{2,1},{3,2},{4,3},{5,4},{6,5},{7,6},{8,7},{9,8},{10,9... | collective-permute-start | bytes 282632 | tf_op jit(solution)/shard_map/ppermute | solution.py:361

commit v3 on v2

--- a/solution.py
+++ b/solution.py
@@ -112,43 +112,49 @@
 
 
 def mixing_rows(hermitian, hermitian_turned):
-    shape = (NVEC, 128)
+    shape = (8, 128)
     lanes, rows = lane_of(shape), row_of(shape)
     lower = lanes < 48
-    lower_row = lower[:1]
-    mix = jnp.where((lanes % 48 == rows) & (lanes < 96), 1.0, 0.0)
-    turned = jnp.where((lanes % 48 == rows + 24) & (lanes < 96), 1.0, 0.0)
-    weights = jnp.ones(shape, F32)
-
-    def spread(column, offset):
-        first = hermitian[:, offset + column : offset + column + 1]
-        second = hermitian[:, 48 + offset + column : 49 + offset + column]
-        return jnp.where(lower, first, second)
+    blocks = range(3)
+
+    def split(value):
+        return [value[8 * block : 8 * block + 8] for block in blocks]
+
+    gram, gram_turned = split(hermitian), split(hermitian_turned)
+    mix = [jnp.where((lanes % 48 == rows + 8 * block) & (lanes < 96), 1.0, 0.0) for block in blocks]
+    turned = [jnp.where((lanes % 48 == rows + 8 * block + 24) & (lanes < 96), 1.0, 0.0) for block in blocks]
+    weights = []
+
+    def spread(value, at):
+        return jnp.where(lower, value[:, at : at + 1], value[:, 48 + at : 49 + at])
 
     for column in range(NVEC):
-        row = hermitian[column : column + 1]
-        row_turned = hermitian_turned[column : column + 1]
-        mix_row = mix[column : column + 1]
-        mix_row_turned = turned[column : column + 1]
+        own, place = column // 8, column % 8
+        here = slice(place, place + 1)
+        row, row_turned = gram[own][here], gram_turned[own][here]
+        mix_row, mix_turned = mix[own][here], turned[own][here]
         product = row * mix_row
-        first = jnp.sum(jnp.where(lower_row, product, 0.0), axis=1, keepdims=True)
-        second = jnp.sum(jnp.where(lower_row, 0.0, product), axis=1, keepdims=True)
-        weight = jnp.where(lower_row, first, second)
-        weights = jnp.where(rows == column, weight, weights)
-        if column == NVEC - 1:
+        both = jnp.concatenate([jnp.where(lower[:1], product, 0.0), jnp.where(lower[:1], 0.0, product)], axis=0)
+        both = jnp.sum(both, axis=1, keepdims=True)
+        weight = jnp.where(lower[:1], both[:1], both[1:])
+        weights.append(weight)
+        active = [block for block in blocks if 8 * block + 7 > column]
+        if not active:
             break
-        ratio = jnp.where(rows > column, TARGET / weight, 0.0)
-        by_re = spread(column, 0) * ratio
-        by_im = spread(column, 24) * ratio
-        hermitian, hermitian_turned = (
-            hermitian - (by_re * row + by_im * row_turned),
-            hermitian_turned - (by_re * row_turned - by_im * row),
-        )
-        mix, turned = (
-            mix - (by_re * mix_row + by_im * mix_row_turned),
-            turned - (by_re * mix_row_turned - by_im * mix_row),
-        )
-    return mix * jnp.sqrt(TARGET / weights)
+        ratio = TARGET / weight
+        for block in active:
+            a_re, a_im = spread(gram[block], column), spread(gram[block], column + 24)
+            scale = jnp.where(rows + 8 * block > column, ratio, 0.0) if block == own else ratio
+            gram_step = a_re * row + a_im * row_turned
+            gram_turned_step = a_re * row_turned - a_im * row
+            mix_step = a_re * mix_row + a_im * mix_turned
+            turned_step = a_re * mix_turned - a_im * mix_row
+            gram[block] = gram[block] - scale * gram_step
+            gram_turned[block] = gram_turned[block] - scale * gram_turned_step
+            mix[block] = mix[block] - scale * mix_step
+            turned[block] = turned[block] - scale * turned_step
+    weights = jnp.concatenate(weights, axis=0)
+    return jnp.concatenate(mix, axis=0) * jnp.sqrt(TARGET / weights)
 
 
 def first_kernel(nn_ref, own_ref, start_ref, mix_ref, py_ref, px_ref, pz_ref):
@@ -191,9 +197,62 @@
     start_ref[...] = every[:, :WIDE]
 
 
-def second_kernel(
-    rx_ref, ry_ref, rz_ref, own_ref, start_ref, mix_ref, ga_ref, code_ref, flat_ref, order_ref
-):
+def hop(gauge, same, turned, sign):
+    moved_re = jnp.zeros((64, WIDE), F32)
+    moved_im = jnp.zeros((64, WIDE), F32)
+    for turn in range(3):
+        u = gauge[:, turn * PAD : turn * PAD + WIDE].astype(F32)
+        v = same.astype(F32) if turn == 0 else turned[:, (turn - 1) * PAD : (turn - 1) * PAD + WIDE]
+        moved_re = moved_re + (u[:64] * v[:64] - u[64:] * v[64:])
+        moved_im = moved_im + (u[:64] * v[64:] + u[64:] * v[:64])
+    if sign < 0:
+        moved_re, moved_im = -moved_re, -moved_im
+    top_re, top_im = moved_re.astype(BF16), moved_im.astype(BF16)
+    low_re = (moved_re - top_re.astype(F32)).astype(BF16)
+    low_im = (moved_im - top_im.astype(F32)).astype(BF16)
+    return (
+        jnp.concatenate([top_re, top_im, low_re, low_im], axis=0),
+        jnp.concatenate([top_im, -top_re, low_im, -low_re], axis=0),
+    )
+
+
+def spin_fold(wide_re, wide_im, direction):
+    group = lane_of((NVEC, WIDE)) // NVEC
+    fold_re, fold_im = [], []
+    for chirality in range(2):
+        sum_re = jnp.zeros((NVEC, WIDE), F32)
+        sum_im = jnp.zeros((NVEC, WIDE), F32)
+        for row_spin, col_spin, value in GAMMA[direction]:
+            if chirality == 1:
+                row_spin, col_spin, value = col_spin, row_spin, np.conj(value)
+            factor = -value
+            for colour in range(3):
+                index = chirality * 6 + row_spin * 3 + colour
+                here = slice(index * NVEC, (index + 1) * NVEC)
+                at_re, at_im = wide_re[here], wide_im[here]
+                if np.imag(factor) != 0:
+                    over_re, over_im = -float(np.imag(factor)) * at_im, float(np.imag(factor)) * at_re
+                else:
+                    over_re, over_im = float(np.real(factor)) * at_re, float(np.real(factor)) * at_im
+                partner = (1 - chirality) * 6 + col_spin * 3 + colour
+                sum_re = jnp.where(group == index, at_re, jnp.where(group == partner, over_re, sum_re))
+                sum_im = jnp.where(group == index, at_im, jnp.where(group == partner, over_im, sum_im))
+        fold_re.append(sum_re)
+        fold_im.append(sum_im)
+    return jnp.concatenate(fold_re + fold_im, axis=0)
+
+
+def link_matrix(folded, spread, left):
+    mix_re = jnp.concatenate([spread[:, :WIDE], spread[:, PAD : PAD + WIDE]], axis=0)
+    mix_im = jnp.concatenate([spread[:, 2 * PAD : 2 * PAD + WIDE], spread[:, 3 * PAD : 3 * PAD + WIDE]], axis=0)
+    by_re = dot(folded, mix_re, ((1,), (1,)), FULL_PRECISION)
+    by_im = dot(folded, mix_im, ((1,), (1,)), FULL_PRECISION)
+    on_re = dot(left, by_re[:48] - by_im[48:], precision=FULL_PRECISION)
+    on_im = dot(left, by_im[:48] + by_re[48:], precision=FULL_PRECISION)
+    return on_re[:48] + on_im[48:], on_im[:48] - on_re[48:]
+
+
+def own_kernel(own_ref, start_ref, mix_ref, ga_ref, gauge_ref, turns_ref, spread_ref, rows_ref, left_ref, last_ref):
     selection = jnp.concatenate(all_rows() + layer_rows(3), axis=0)
     face_links = dot(selection, ga_ref[...]).astype(BF16)
     picked = dot(face_links, link_pick()).astype(BF16)
@@ -205,92 +264,56 @@
                 piece = axis * 4 + step
                 link_rows.append(picked[first + 16 * part : first + 16 * part + 16, piece * 128 : piece * 128 + 16])
     link_rows.append(picked[:128, 12 * 128 : 12 * 128 + 16])
-    gauge = dot(jnp.concatenate(link_rows, axis=0), link_spread())
-    ahead = []
-    for ref in (rx_ref, ry_ref, rz_ref):
-        face = jnp.concatenate([ref[column * 32 : column * 32 + 32, :] for column in range(9)], axis=1)
-        ahead.append(time_rows(face[:16]))
-        ahead.append(time_rows(face[16:]))
-    ahead.append(start_ref[...])
-    ahead = jnp.concatenate(ahead, axis=0)
-    turned = dot(ahead, colour_turns())
-    same = ahead.astype(F32)
-    shifted = [same, turned[:, :WIDE], turned[:, PAD : PAD + WIDE]]
+    gauge = dot(jnp.concatenate(link_rows, axis=0), link_spread()).astype(BF16)
+    gauge_ref[...] = gauge[:384]
+    turns = colour_turns()
+    turns_ref[...] = turns
+    spread_matrix = mixing_spread()
+    spread_ref[...] = spread_matrix
+    mix = mix_ref[...]
+    zero = jnp.zeros((NVEC, NVEC), F32)
+    left = []
+    for part in range(2):
+        first = mix[:, part * 24 : part * 24 + 24]
+        second = mix[:, 48 + part * 24 : 72 + part * 24]
+        left += [jnp.concatenate([first, zero], axis=1), jnp.concatenate([zero, second], axis=1)]
+    left = jnp.concatenate(left, axis=0)
+    left_ref[...] = left
+    for axis in range(3):
+        mine = own_ref[axis]
+        rows_ref[axis] = jnp.concatenate([mine, mine], axis=0).T
+    mine = own_ref[3]
+    rows = jnp.concatenate([mine, mine], axis=0).T
+    start = start_ref[...]
+    to_re, to_im = hop(gauge[384:], start, dot(start, turns), -1.0)
+    folded = spin_fold(dot(rows, to_re), dot(rows, to_im), 3)
+    spread = dot(mix, spread_matrix, precision=FULL_PRECISION)
+    last_re, last_im = link_matrix(folded, spread, left)
+    last_ref[:48, :] = last_re
+    last_ref[48:, :] = last_im
+
+
+def second_kernel(
+    rx_ref, ry_ref, rz_ref, gauge_ref, turns_ref, spread_ref, rows_ref, left_ref, last_ref, code_ref, flat_ref, order_ref
+):
+    flat_ref[288:, :] = last_ref[...]
+    left = left_ref[...]
     mixings = []
     for ref in (rx_ref, ry_ref, rz_ref):
         parts = ref[MIX_ROW:SENT, :].astype(F32)
         mixings.append(parts[48:72] + parts[24:48] + parts[:24])
-    mixings.append(mix_ref[...])
-    spread = dot(jnp.concatenate(mixings, axis=0), mixing_spread(), precision=FULL_PRECISION)
-    own_mix = mix_ref[...]
-    group = lane_of((NVEC, WIDE)) // NVEC
-    halves = []
-    for direction in range(4):
+    spread = dot(jnp.concatenate(mixings, axis=0), spread_ref[...], precision=FULL_PRECISION)
+    for direction, ref in enumerate((rx_ref, ry_ref, rz_ref)):
+        face = jnp.concatenate([ref[column * 32 : column * 32 + 32, :] for column in range(9)], axis=1)
+        ahead = jnp.concatenate([time_rows(face[:16]), time_rows(face[16:])], axis=0)
+        turned = dot(ahead, turns_ref[...])
         base = direction * 128
-        sign = -1.0 if direction == 3 else 1.0
-        moved_re = jnp.zeros((64, WIDE), F32)
-        moved_im = jnp.zeros((64, WIDE), F32)
-        for turn in range(3):
-            lanes = slice(turn * PAD, turn * PAD + WIDE)
-            u_re = gauge[base : base + 64, lanes]
-            u_im = gauge[base + 64 : base + 128, lanes]
-            v_re = shifted[turn][base : base + 64]
-            v_im = shifted[turn][base + 64 : base + 128]
-            moved_re = moved_re + (u_re * v_re - u_im * v_im)
-            moved_im = moved_im + (u_re * v_im + u_im * v_re)
-        if sign < 0:
-            moved_re, moved_im = -moved_re, -moved_im
-        top_re = moved_re.astype(BF16)
-        top_im = moved_im.astype(BF16)
-        low_re = (moved_re - top_re.astype(F32)).astype(BF16)
-        low_im = (moved_im - top_im.astype(F32)).astype(BF16)
-        mine = own_ref[direction]
-        mine = jnp.concatenate([mine, mine], axis=0)
-        wide_re = dot(mine, jnp.concatenate([top_re, top_im, low_re, low_im], axis=0), ((0,), (0,)))
-        wide_im = dot(mine, jnp.concatenate([top_im, -top_re, low_im, -low_re], axis=0), ((0,), (0,)))
-        fold_re, fold_im = [], []
-        for chirality in range(2):
-            sum_re = jnp.zeros((NVEC, WIDE), F32)
-            sum_im = jnp.zeros((NVEC, WIDE), F32)
-            for row_spin, col_spin, value in GAMMA[direction]:
-                if chirality == 1:
-                    row_spin, col_spin, value = col_spin, row_spin, np.conj(value)
-                factor = -value
-                for colour in range(3):
-                    index = chirality * 6 + row_spin * 3 + colour
-                    here = slice(index * NVEC, (index + 1) * NVEC)
-                    at_re, at_im = wide_re[here], wide_im[here]
-                    if np.imag(factor) != 0:
-                        over_re, over_im = -float(np.imag(factor)) * at_im, float(np.imag(factor)) * at_re
-                    else:
-                        over_re, over_im = float(np.real(factor)) * at_re, float(np.real(factor)) * at_im
-                    partner = (1 - chirality) * 6 + col_spin * 3 + colour
-                    sum_re = jnp.where(group == index, at_re, jnp.where(group == partner, over_re, sum_re))
-                    sum_im = jnp.where(group == index, at_im, jnp.where(group == partner, over_im, sum_im))
-            fold_re.append(sum_re)
-            fold_im.append(sum_im)
-        folded = jnp.concatenate(fold_re + fold_im, axis=0)
-        rows = slice(direction * NVEC, (direction + 1) * NVEC)
-        mix_re = jnp.concatenate([spread[rows, :WIDE], spread[rows, PAD : PAD + WIDE]], axis=0)
-        mix_im = jnp.concatenate([spread[rows, 2 * PAD : 2 * PAD + WIDE], spread[rows, 3 * PAD : 3 * PAD + WIDE]], axis=0)
-        by_re = dot(folded, mix_re, ((1,), (1,)), FULL_PRECISION)
-        by_im = dot(folded, mix_im, ((1,), (1,)), FULL_PRECISION)
-        halves.append((by_re[:48] - by_im[48:], by_im[:48] + by_re[48:]))
-    square = (NVEC, 48)
-    zero = jnp.zeros((NVEC, NVEC), F32)
-    left_re = jnp.concatenate(
-        [jnp.concatenate([own_mix[:, 0:24], zero], axis=1), jnp.concatenate([zero, own_mix[:, 48:72]], axis=1)], axis=0
-    )
-    left_im = jnp.concatenate(
-        [jnp.concatenate([own_mix[:, 24:48], zero], axis=1), jnp.concatenate([zero, own_mix[:, 72:96]], axis=1)], axis=0
-    )
-    left = jnp.concatenate([left_re, left_im], axis=0)
-    for direction in range(4):
-        half_re, half_im = halves[direction]
-        on_re = dot(left, half_re, precision=FULL_PRECISION)
-        on_im = dot(left, half_im, precision=FULL_PRECISION)
-        flat_ref[direction * 96 : direction * 96 + 48, :] = on_re[:48] + on_im[48:]
-        flat_ref[direction * 96 + 48 : direction * 96 + 96, :] = on_im[:48] - on_re[48:]
+        to_re, to_im = hop(gauge_ref[base : base + 128, :], ahead, turned, 1.0)
+        rows = rows_ref[direction]
+        folded = spin_fold(dot(rows, to_re), dot(rows, to_im), direction)
+        y_re, y_im = link_matrix(folded, spread[direction * NVEC : (direction + 1) * NVEC], left)
+        flat_ref[direction * 96 : direction * 96 + 48, :] = y_re
+        flat_ref[direction * 96 + 48 : direction * 96 + 96, :] = y_im
     pieces = [flat_ref[pl.ds(row, 48, stride=8), :] for row in range(8)]
     long = jnp.concatenate(pieces, axis=1)
     for direction in range(4):
@@ -312,14 +335,20 @@
     code_ref[144:160, :] = powers.astype(jnp.int32).astype(jnp.int16)
 
 
-def place_kernel(order, site_ref, code_ref, out_ref):
+def place_kernel(order, site_ref, code_ref, out_ref, wide_ref, sem_ref):
+    copies = []
     for index in range(COUNT):
-        target = site_ref[0, order[index]]
         power = code_ref[index, 144:160, :].astype(jnp.int32).astype(F32)
         scale = jnp.exp2(power) * (1.0 / 32767.0)
         for block in range(9):
             values = code_ref[index, block * 16 : block * 16 + 16, :].astype(jnp.int32).astype(F32)
-            out_ref[target, block * 16 : block * 16 + 16, :] = values * scale[block : block + 1]
+            wide_ref[index, block * 16 : block * 16 + 16, :] = values * scale[block : block + 1]
+        target = site_ref[0, order[index]]
+        copy = pltpu.make_async_copy(wide_ref.at[index], out_ref.at[target], sem_ref.at[index])
+        copy.start()
+        copies.append(copy)
+    for copy in copies:
+        copy.wait()
 
 
 def first_call(block):
@@ -336,21 +365,40 @@
     )(block)
 
 
-def second_call(faces, own, start, mix, gauge):
+def own_call(own, start, mix, gauge):
+    return pl.pallas_call(
+        own_kernel,
+        out_shape=[
+            jax.ShapeDtypeStruct((384, 3 * PAD), BF16),
+            jax.ShapeDtypeStruct((WIDE, 2 * PAD), BF16),
+            jax.ShapeDtypeStruct((128, 4 * PAD), F32),
+            jax.ShapeDtypeStruct((3, WIDE, 256), BF16),
+            jax.ShapeDtypeStruct((96, 48), F32),
+            jax.ShapeDtypeStruct((96, 48), F32),
+        ],
+        compiler_params=pltpu.CompilerParams(vmem_limit_bytes=40 * 2**20),
+        cost_estimate=pl.CostEstimate(flops=2 * 10**9, bytes_accessed=4 * 10**6, transcendentals=0),
+        name="own_part",
+    )(own, start, mix, gauge)
+
+
+def second_call(faces, prepared):
     return pl.pallas_call(
         second_kernel,
         out_shape=jax.ShapeDtypeStruct((160, 128), jnp.int16),
         scratch_shapes=[pltpu.VMEM((384, 48), F32), pltpu.VMEM((144, 128), F32)],
         compiler_params=pltpu.CompilerParams(vmem_limit_bytes=40 * 2**20),
         name="coarse_links",
-    )(*faces, own, start, mix, gauge)
+    )(*faces, *prepared)
 
 
 def place_call(site_map, codes, order):
     return pl.pallas_call(
-        lambda site_ref, code_ref, out_ref: place_kernel(order, site_ref, code_ref, out_ref),
+        lambda *refs: place_kernel(order, *refs),
         in_specs=[pl.BlockSpec(memory_space=pltpu.SMEM), pl.BlockSpec(memory_space=pltpu.VMEM)],
+        out_specs=pl.BlockSpec(memory_space=pl.ANY),
         out_shape=jax.ShapeDtypeStruct((COUNT, 144, 128), F32),
+        scratch_shapes=[pltpu.VMEM((COUNT, 144, 128), F32), pltpu.SemaphoreType.DMA((COUNT,))],
         compiler_params=pltpu.CompilerParams(vmem_limit_bytes=40 * 2**20),
         name="place_links",
     )(site_map, codes)
@@ -379,7 +427,8 @@
     face_y = passed_back(face_y, "gy")
     face_x = passed_back(face_x, "gx")
     face_z = passed_back(face_z, "zt")
-    code = second_call((face_x, face_y, face_z), own, start, mix, gauge.reshape(2 * SITES, LINKS))
+    prepared = own_call(own, start, mix, gauge.reshape(2 * SITES, LINKS))
+    code = second_call((face_x, face_y, face_z), prepared)
     codes, order = gathered(code)
     placed = place_call(site_map, codes, order)
     placed = placed.reshape(COUNT, 72, 2, 128).transpose(0, 2, 1, 3)

time: 69.7 us -> 68.8 us (0.987)
  waiting for transfers between devices: 2.09 us -> 0.01 us
  Pallas kernels: 11.2 us -> 12.2 us
    pallas_call x1 -> x2, Pallas kernels: 2.25 us -> 4.53 us  [the longest x1 2.31 us: own_call(): pl.pallas_call(own_kernel, out_shape=[jax.ShapeDtypeStruct((384, 3 * PAD)...]
    ppermute x3, waiting for transfers between devices: 2.09 us -> 0.01 us  [passed_back(): lax.ppermute(value, axis, [(source, (source - 1) % count) for source in r...]
    pallas_call x1, Pallas kernels: 4.45 us -> 3.71 us  [first_call(): pl.pallas_call(first_kernel, out_shape=[jax.ShapeDtypeStruct((4, 128, WID...]
  transfers between devices with their start and end apart: 3 -> 3, of which waited for: 1 -> 0; matrix products, arithmetic and copies ran while one was open for 1% -> 1% of each run, Pallas kernels for 0% -> 3%
where the time goes in v3:
time: 68.8 us; the launch traced here: 68.5 us
  blocking collectives  37.4 us (54%)
  starting transfers between devices  16.8 us (24%)
  Pallas kernels  12.2 us (18%)
  local copies, waits for them, and re-layouts  1.98 us (3%)
    all_gather x1, blocking collectives, gathered(): lax.all_gather(code, names, axis=0, tiled=True, axis_index_groups=rings)  33.9 us
    ppermute x3, starting transfers between devices, passed_back(): lax.ppermute(value, axis, [(source, (source - 1) % count) for source in r...  16.8 us
    pallas_call x1, Pallas kernels, second_call(): pl.pallas_call(second_kernel, out_shape=jax.ShapeDtypeStruct((160, 128),...  3.99 us
    pallas_call x1, Pallas kernels, first_call(): pl.pallas_call(first_kernel, out_shape=[jax.ShapeDtypeStruct((4, 128, WID...  3.71 us
    all_gather x1, blocking collectives, gathered(): lax.all_gather(code[None], names, axis=0, tiled=True, axis_index_groups=p...  3.53 us
    pallas_call x1, Pallas kernels, own_call(): pl.pallas_call(own_kernel, out_shape=[jax.ShapeDtypeStruct((384, 3 * PAD)...  2.31 us
    pallas_call x1, Pallas kernels, place_call(): pl.pallas_call(lambda *refs: place_kernel(order, *refs), in_specs=[pl.Blo...  2.22 us
  transfers between devices with their start and end apart: 3, of which 0 were waited for; matrix products, arithmetic and copies ran while one was open for 1% of the time, Pallas kernels for 3%

profile of v3, /device:TPU:1, one launch (start us, length us, event | category | flops | bytes accessed | tf_op | source)
XLA Modules:
  0.0 68.5 jit_solution(13922871005083483914)
XLA Ops:
  0.0 1.1 %reshape.12.nn_ref = bf16[128,1152]{1,0:T(8,128)(2,1)S(1)} reshape(bf16[4,4,4,2,1152]{4,3,2,1,0:T(2,128)(2,1)} %param.3) | data formatting | bytes 589824 | tf_op jit(solution)/shard_map/reshape | solution.py:426
  1.1 3.7 %gram_and_mixing.1 = (bf16[4,128,288]{2,1,0:T(8,128)(2,1)S(1)}, bf16[128,288]{1,0:T(8,128)(2,1)S(1)}, f32[24,128]{1,0:T(8,128)S(1)}, bf16[368,128]{1,0:T(8,128)(...) custom-call(bf16[128,1152]{1,0:T(8,128)(2,1)S(1)} %reshape.12.nn_ref), custom_call_target="tpu_custom_call" | custom-call | tf_op jit(solution)/shard_map/gram_and_mixing/pallas_call | solution.py:355
  4.8 7.1 %collective-permute-start = (bf16[368,128]{1,0:T(8,128)(2,1)S(1)}, bf16[368,128]{1,0:T(8,128)(2,1)S(1)}, u32[]{:S(2)}, u32[]{:S(2)}) collective-permute-start(bf16[368,128]{1,0:T(8,128)(2,1)S(1)} %get-tuple-element.17), channel_id=1, source_target_pairs={{0,384},{128,0},{256,128},{384,256},{1,385},{129,1},{257,129},{385... | collective-permute-start | bytes 282632 | tf_op jit(solution)/shard_map/ppermute | solution.py:409
  11.9 3.6 %collective-permute-start.1 = (bf16[368,128]{1,0:T(8,128)(2,1)S(1)}, bf16[368,128]{1,0:T(8,128)(2,1)S(1)}, u32[]{:S(2)}, u32[]{:S(2)}) collective-permute-start(bf16[368,128]{1,0:T(8,128)(2,1)S(1)} %get-tuple-element.18), channel_id=1, source_target_pairs={{0,112},{16,0},{32,16},{48,32},{64,48},{80,64},{96,80},{112,96},{1... | collective-permute-start | bytes 282632 | tf_op jit(solution)/shard_map/ppermute | solution.py:409
  15.5 6.1 %collective-permute-start.2 = (bf16[368,128]{1,0:T(8,128)(2,1)S(1)}, bf16[368,128]{1,0:T(8,128)(2,1)S(1)}, u32[]{:S(2)}, u32[]{:S(2)}) collective-permute-start(bf16[368,128]{1,0:T(8,128)(2,1)S(1)} %get-tuple-element.19), channel_id=1, source_target_pairs={{0,15},{1,0},{2,1},{3,2},{4,3},{5,4},{6,5},{7,6},{8,7},{9,8},{10,9... | collective-permute-start | bytes 282632 | tf_op jit(solution)/shard_map/ppermute | solution.py:409
  21.6 0.9 %reshape.13.ga_ref = bf16[128,144]{1,0:T(8,128)(2,1)S(1)} reshape(bf16[4,4,4,2,144]{4,3,2,1,0:T(2,128)(2,1)} %param.4) | data formatting | bytes 73728 | tf_op jit(solution)/shard_map/reshape | solution.py:430
  22.5 2.3 %own_part.1 = (bf16[384,1152]{1,0:T(8,128)(2,1)S(1)}, bf16[288,768]{1,0:T(8,128)(2,1)S(1)}, f32[128,1536]{1,0:T(8,128)S(1)}, bf16[3,288,256]{2,1,0:T(8,128)(2,1)...) custom-call(bf16[4,128,288]{2,1,0:T(8,128)(2,1)S(1)} %get-tuple-element.20.own_ref, ...), custom_call_target="tpu_custom_call" | custom-call | flops 2000000000 | bytes 4000000 | tf_op jit(solution)/shard_map/own_part/pallas_call | solution.py:369
  24.8 0.0 copy-start
  24.8 0.0 collective-permute-done.rx_ref
  24.9 0.0 collective-permute-done.1.ry_ref
  24.9 0.0 collective-permute-done.2.rz_ref
  24.9 4.0 %coarse_links.1 = s16[160,128]{1,0:T(8,128)(2,1)S(1)} custom-call(bf16[368,128]{1,0:T(8,128)(2,1)S(1)} %collective-permute-done.rx_ref, bf16[368,128]{1,0:T(8,128)(2,1)S(1)} %collective-permute-done.1.ry_ref, bf16[368,128]{1,0:T(8,128)(2,1)S(1)} %collective-permute-done.2.rz_ref, bf16[384,1152]{1,0:T(8,128)(2,1)S(1)} %get-tuple-element.23.gauge_ref, ...), custom_call_target="tpu_custom_call" | custom-call | tf_op jit(solution)/shard_map/coarse_links/pallas_call | solution.py:386
  28.9 3.5 %all-gather = s16[320,128]{1,0:T(8,128)(2,1)S(1)} all-gather(s16[160,128]{1,0:T(8,128)(2,1)S(1)} %coarse_links.1), channel_id=2, replica_groups={{0,128},{16,144},{256,384},{272,400},{32,160},{48,176},{288,416},{304,4..., dimensions={0}, use_global_device_ids=true | all-gather | bytes 122880 | tf_op jit(solution)/shard_map/all_gather | solution.py:420
  32.4 33.9 %all-gather.2.refs_1_ = s16[32,160,128]{2,1,0:T(8,128)(2,1)S(1)} all-gather(s16[2,160,128]{2,1,0:T(8,128)(2,1)S(1)} %bitcast.6), channel_id=1, replica_groups={{0,16,256,272,32,48,288,304,64,80,320,336,96,112,352,368},{128,144,384,..., dimensions={0}, use_global_device_ids=true | all-gather | bytes 1392640 | tf_op jit(solution)/shard_map/all_gather | solution.py:421
  66.3 0.0 copy-done
  66.3 2.2 %place_links.1 = f32[32,144,128]{2,1,0:T(8,128)} custom-call(s32[1,32]{1,0:T(1,128)S(1)} %copy-done, s16[32,160,128]{2,1,0:T(8,128)(2,1)S(1)} %all-gather.2.refs_1_), custom_call_target="tpu_custom_call" | custom-call | tf_op jit(solution)/shard_map/place_links/pallas_call | solution.py:396
Async XLA Ops:
  4.8 20.0 %collective-permute-start = (bf16[368,128]{1,0:T(8,128)(2,1)S(1)}, bf16[368,128]{1,0:T(8,128)(2,1)S(1)}, u32[]{:S(2)}, u32[]{:S(2)}) collective-permute-start(bf16[368,128]{1,0:T(8,128)(2,1)S(1)} %get-tuple-element.17), channel_id=1, source_target_pairs={{0,384},{128,0},{256,128},{384,256},{1,385},{129,1},{257,129},{385... | collective-permute-start | bytes 282632 | tf_op jit(solution)/shard_map/ppermute | solution.py:409
  11.9 13.0 %collective-permute-start.1 = (bf16[368,128]{1,0:T(8,128)(2,1)S(1)}, bf16[368,128]{1,0:T(8,128)(2,1)S(1)}, u32[]{:S(2)}, u32[]{:S(2)}) collective-permute-start(bf16[368,128]{1,0:T(8,128)(2,1)S(1)} %get-tuple-element.18), channel_id=1, source_target_pairs={{0,112},{16,0},{32,16},{48,32},{64,48},{80,64},{96,80},{112,96},{1... | collective-permute-start | bytes 282632 | tf_op jit(solution)/shard_map/ppermute | solution.py:409
  15.5 9.3 %collective-permute-start.2 = (bf16[368,128]{1,0:T(8,128)(2,1)S(1)}, bf16[368,128]{1,0:T(8,128)(2,1)S(1)}, u32[]{:S(2)}, u32[]{:S(2)}) collective-permute-start(bf16[368,128]{1,0:T(8,128)(2,1)S(1)} %get-tuple-element.19), channel_id=1, source_target_pairs={{0,15},{1,0},{2,1},{3,2},{4,3},{5,4},{6,5},{7,6},{8,7},{9,8},{10,9... | collective-permute-start | bytes 282632 | tf_op jit(solution)/shard_map/ppermute | solution.py:409
  24.8 41.5 %copy-start = (s32[1,32]{1,0:T(1,128)S(1)}, s32[1,32]{1,0:T(1,128)}, u32[]{:S(2)}) copy-start(s32[1,32]{1,0:T(1,128)} %refs_0_.1) | copy-start | bytes 388

commit v4 on v3

--- a/solution.py
+++ b/solution.py
@@ -17,10 +17,10 @@
 FULL = 4 * WIDE
 LINKS = 144
 COUNT = 32
+CHUNK = 4
 MIX_ROW = 288
-SENT = 368
+SENT = 336
 TARGET = 64.0
-FULL_PRECISION = lax.Precision.HIGHEST
 GAMMA = [
     ((0, 1, -1j), (1, 0, -1j)),
     ((0, 1, -1), (1, 0, 1)),
@@ -29,8 +29,26 @@
 ]
 
 
-def dot(left, right, dims=((1,), (0,)), precision=None):
-    return lax.dot_general(left, right, (dims, ((), ())), precision=precision, preferred_element_type=F32)
+def dot(left, right, dims=((1,), (0,))):
+    return lax.dot_general(left, right, (dims, ((), ())), preferred_element_type=F32)
+
+
+def bf16_parts(value, count):
+    parts = []
+    for _ in range(count):
+        part = value.astype(BF16)
+        parts.append(part)
+        value = value - part.astype(F32)
+    return parts
+
+
+def dot_parts(parts, ones):
+    rows = parts[0].shape[0]
+    out = dot(jnp.concatenate(parts, axis=0), ones)
+    total = out[(len(parts) - 1) * rows :]
+    for index in reversed(range(len(parts) - 1)):
+        total = total + out[index * rows : (index + 1) * rows]
+    return total
 
 
 def time_rows(block):
@@ -66,7 +84,7 @@
     shape = (WIDE, 128)
     rows = row_of(shape)
     away = lane_of(shape) - ((rows // 144) * 48 + rows % NVEC)
-    return jnp.concatenate([ones_where(away == part * NVEC, F32) for part in range(2)], axis=1)
+    return jnp.concatenate([ones_where(away == part * NVEC, BF16) for part in range(2)], axis=1)
 
 
 def mixing_spread():
@@ -77,7 +95,7 @@
         for chirality in range(2):
             inside = (lanes >= chirality * 144) & (lanes < chirality * 144 + 144)
             source = jnp.where(inside, lanes % NVEC + chirality * 48 + part * NVEC, -1)
-            blocks.append(ones_where(rows == source, F32))
+            blocks.append(ones_where(rows == source, BF16))
     return jnp.concatenate(blocks, axis=1)
 
 
@@ -172,18 +190,12 @@
         here = slice(index * NVEC, (index + 1) * NVEC)
         fold_re = jnp.where(group == index, wide_re[here], fold_re)
         fold_im = jnp.where(group == index, wide_im[here], fold_im)
-    folded = dot(jnp.concatenate([fold_re, fold_im], axis=0), gram_fold(), precision=FULL_PRECISION)
+    folded = dot_parts(bf16_parts(jnp.concatenate([fold_re, fold_im], axis=0), 3), gram_fold())
     hermitian = folded[:NVEC, :128] - folded[NVEC:, 128:]
     hermitian_turned = folded[NVEC:, :128] + folded[:NVEC, 128:]
     mix = mixing_rows(hermitian, hermitian_turned)
     mix_ref[...] = mix
-    parts = []
-    rest = mix
-    for _ in range(3):
-        part = rest.astype(BF16).astype(F32)
-        parts.append(part)
-        rest = rest - part
-    packed = jnp.concatenate(parts + [jnp.zeros((8, 128), F32)], axis=0).astype(BF16)
+    packed = jnp.concatenate(bf16_parts(mix, 2), axis=0)
     for axis, out in enumerate((px_ref, py_ref, pz_ref)):
         first = 224 + 32 * axis
         for column in range(9):
@@ -242,17 +254,57 @@
     return jnp.concatenate(fold_re + fold_im, axis=0)
 
 
-def link_matrix(folded, spread, left):
-    mix_re = jnp.concatenate([spread[:, :WIDE], spread[:, PAD : PAD + WIDE]], axis=0)
-    mix_im = jnp.concatenate([spread[:, 2 * PAD : 2 * PAD + WIDE], spread[:, 3 * PAD : 3 * PAD + WIDE]], axis=0)
-    by_re = dot(folded, mix_re, ((1,), (1,)), FULL_PRECISION)
-    by_im = dot(folded, mix_im, ((1,), (1,)), FULL_PRECISION)
-    on_re = dot(left, by_re[:48] - by_im[48:], precision=FULL_PRECISION)
-    on_im = dot(left, by_im[:48] + by_re[48:], precision=FULL_PRECISION)
-    return on_re[:48] + on_im[48:], on_im[:48] - on_re[48:]
-
-
-def own_kernel(own_ref, start_ref, mix_ref, ga_ref, gauge_ref, turns_ref, spread_ref, rows_ref, left_ref, last_ref):
+def spread_mixing(parts, ones):
+    rows = parts[0].shape[0]
+    out = dot(jnp.concatenate(parts, axis=0), ones).astype(BF16)
+    gap = jnp.zeros((80, WIDE), BF16)
+    result = []
+    for first in range(0, rows, NVEC):
+        pair = []
+        for index in range(2):
+            here = slice(index * rows + first, index * rows + first + NVEC)
+            blocks = [out[here, block * PAD : block * PAD + WIDE] for block in range(4)]
+            pair.append(jnp.concatenate([blocks[0], blocks[1], gap, blocks[2], blocks[3]], axis=0))
+        result.append(pair)
+    return result
+
+
+def link_matrix(folded, mixing, left):
+    top, low = bf16_parts(folded, 2)
+    by = dot(jnp.concatenate([top, low], axis=0), mixing[0], ((1,), (1,)))
+    by = by[:96] + (by[96:] + dot(top, mixing[1], ((1,), (1,))))
+    by_re, by_im = by[:, :48], by[:, 128:]
+    half = jnp.concatenate([by_re[:48] - by_im[48:], jnp.zeros((48, 80), F32), by_im[:48] + by_re[48:]], axis=1)
+    top, low = bf16_parts(half, 2)
+    on = dot(left, top)
+    on = on[:96] + (on[96:] + dot(left[:96], low))
+    return on[:48, :48] + on[48:, 128:], on[:48, 128:] - on[48:, :48]
+
+
+def next_face(ref):
+    face = jnp.concatenate([ref[column * 32 : column * 32 + 32, :] for column in range(9)], axis=1)
+    parts = ref[MIX_ROW:SENT, :].astype(F32)
+    parts = [parts[:NVEC].astype(BF16), parts[NVEC:].astype(BF16)]
+    return jnp.concatenate([time_rows(face[:16]), time_rows(face[16:])], axis=0), parts
+
+
+def write_rows(links, flat_ref, order_ref):
+    count = 12 * len(links)
+    for index, (_, matrix_re, matrix_im) in enumerate(links):
+        flat_ref[index * 96 : index * 96 + 48, :] = matrix_re
+        flat_ref[index * 96 + 48 : index * 96 + 96, :] = matrix_im
+    long = jnp.concatenate([flat_ref[pl.ds(row, count, stride=8), :] for row in range(8)], axis=1)
+    for index, (direction, _, _) in enumerate(links):
+        for part in range(2):
+            first = (index * 2 + part) * 6
+            for third in range(3):
+                target = direction * 36 + third * 2 + part
+                order_ref[pl.ds(target, 6, stride=6), :] = long[first : first + 6, third * 128 : (third + 1) * 128]
+
+
+def own_kernel(
+    rx_ref, own_ref, start_ref, mix_ref, ga_ref, gauge_ref, turns_ref, spread_ref, rows_ref, left_ref, order_ref, flat_ref
+):
     selection = jnp.concatenate(all_rows() + layer_rows(3), axis=0)
     face_links = dot(selection, ga_ref[...]).astype(BF16)
     picked = dot(face_links, link_pick()).astype(BF16)
@@ -265,7 +317,7 @@
                 link_rows.append(picked[first + 16 * part : first + 16 * part + 16, piece * 128 : piece * 128 + 16])
     link_rows.append(picked[:128, 12 * 128 : 12 * 128 + 16])
     gauge = dot(jnp.concatenate(link_rows, axis=0), link_spread()).astype(BF16)
-    gauge_ref[...] = gauge[:384]
+    gauge_ref[...] = gauge[128:384]
     turns = colour_turns()
     turns_ref[...] = turns
     spread_matrix = mixing_spread()
@@ -277,51 +329,46 @@
         first = mix[:, part * 24 : part * 24 + 24]
         second = mix[:, 48 + part * 24 : 72 + part * 24]
         left += [jnp.concatenate([first, zero], axis=1), jnp.concatenate([zero, second], axis=1)]
-    left = jnp.concatenate(left, axis=0)
+    left = jnp.concatenate(bf16_parts(jnp.concatenate(left, axis=0), 2), axis=0)
     left_ref[...] = left
-    for axis in range(3):
+    rows = []
+    for axis in range(4):
         mine = own_ref[axis]
-        rows_ref[axis] = jnp.concatenate([mine, mine], axis=0).T
-    mine = own_ref[3]
-    rows = jnp.concatenate([mine, mine], axis=0).T
-    start = start_ref[...]
-    to_re, to_im = hop(gauge[384:], start, dot(start, turns), -1.0)
-    folded = spin_fold(dot(rows, to_re), dot(rows, to_im), 3)
-    spread = dot(mix, spread_matrix, precision=FULL_PRECISION)
-    last_re, last_im = link_matrix(folded, spread, left)
-    last_ref[:48, :] = last_re
-    last_ref[48:, :] = last_im
+        rows.append(jnp.concatenate([mine, mine], axis=0).T)
+    rows_ref[0] = rows[1]
+    rows_ref[1] = rows[2]
+    face, mix_x = next_face(rx_ref)
+    ahead = jnp.concatenate([face, start_ref[...]], axis=0)
+    turned = dot(ahead, turns)
+    mixings = spread_mixing([jnp.concatenate(pair, axis=0) for pair in zip(mix_x, bf16_parts(mix, 2))], spread_matrix)
+    links = []
+    for index, direction in enumerate((0, 3)):
+        here = slice(index * 128, index * 128 + 128)
+        to_re, to_im = hop(gauge[direction * 128 : direction * 128 + 128], ahead[here], turned[here], 1.0 - 2.0 * index)
+        folded = spin_fold(dot(rows[direction], to_re), dot(rows[direction], to_im), direction)
+        links.append((direction, *link_matrix(folded, mixings[index], left)))
+    order_ref[...] = jnp.zeros((144, 128), F32)
+    write_rows(links, flat_ref, order_ref)
 
 
 def second_kernel(
-    rx_ref, ry_ref, rz_ref, gauge_ref, turns_ref, spread_ref, rows_ref, left_ref, last_ref, code_ref, flat_ref, order_ref
+    ry_ref, rz_ref, gauge_ref, turns_ref, spread_ref, rows_ref, left_ref, start_ref, code_ref, flat_ref, order_ref
 ):
-    flat_ref[288:, :] = last_ref[...]
+    order_ref[...] = start_ref[...]
     left = left_ref[...]
-    mixings = []
-    for ref in (rx_ref, ry_ref, rz_ref):
-        parts = ref[MIX_ROW:SENT, :].astype(F32)
-        mixings.append(parts[48:72] + parts[24:48] + parts[:24])
-    spread = dot(jnp.concatenate(mixings, axis=0), spread_ref[...], precision=FULL_PRECISION)
-    for direction, ref in enumerate((rx_ref, ry_ref, rz_ref)):
-        face = jnp.concatenate([ref[column * 32 : column * 32 + 32, :] for column in range(9)], axis=1)
-        ahead = jnp.concatenate([time_rows(face[:16]), time_rows(face[16:])], axis=0)
-        turned = dot(ahead, turns_ref[...])
-        base = direction * 128
-        to_re, to_im = hop(gauge_ref[base : base + 128, :], ahead, turned, 1.0)
-        rows = rows_ref[direction]
+    face_y, mix_y = next_face(ry_ref)
+    face_z, mix_z = next_face(rz_ref)
+    ahead = jnp.concatenate([face_y, face_z], axis=0)
+    turned = dot(ahead, turns_ref[...])
+    mixings = spread_mixing([jnp.concatenate(pair, axis=0) for pair in zip(mix_y, mix_z)], spread_ref[...])
+    links = []
+    for index, direction in enumerate((1, 2)):
+        here = slice(index * 128, index * 128 + 128)
+        to_re, to_im = hop(gauge_ref[here, :], ahead[here], turned[here], 1.0)
+        rows = rows_ref[index]
         folded = spin_fold(dot(rows, to_re), dot(rows, to_im), direction)
-        y_re, y_im = link_matrix(folded, spread[direction * NVEC : (direction + 1) * NVEC], left)
-        flat_ref[direction * 96 : direction * 96 + 48, :] = y_re
-        flat_ref[direction * 96 + 48 : direction * 96 + 96, :] = y_im
-    pieces = [flat_ref[pl.ds(row, 48, stride=8), :] for row in range(8)]
-    long = jnp.concatenate(pieces, axis=1)
-    for direction in range(4):
-        for part in range(2):
-            first = (direction * 2 + part) * 6
-            for third in range(3):
-                target = direction * 36 + third * 2 + part
-                order_ref[pl.ds(target, 6, stride=6), :] = long[first : first + 6, third * 128 : (third + 1) * 128]
+        links.append((direction, *link_matrix(folded, mixings[index], left)))
+    write_rows(links, flat_ref, order_ref)
     powers = []
     for block in range(9):
         values = order_ref[block * 16 : block * 16 + 16, :]
@@ -335,18 +382,22 @@
     code_ref[144:160, :] = powers.astype(jnp.int32).astype(jnp.int16)
 
 
-def place_kernel(order, site_ref, code_ref, out_ref, wide_ref, sem_ref):
+def place_kernel(order, site_ref, code_ref, out_ref, wide_ref, source_ref, sem_ref):
+    for index in range(COUNT):
+        source_ref[site_ref[0, order[index]]] = index
     copies = []
-    for index in range(COUNT):
-        power = code_ref[index, 144:160, :].astype(jnp.int32).astype(F32)
+    for site in range(COUNT):
+        source = source_ref[site]
+        power = code_ref[source, 144:160, :].astype(jnp.int32).astype(F32)
         scale = jnp.exp2(power) * (1.0 / 32767.0)
         for block in range(9):
-            values = code_ref[index, block * 16 : block * 16 + 16, :].astype(jnp.int32).astype(F32)
-            wide_ref[index, block * 16 : block * 16 + 16, :] = values * scale[block : block + 1]
-        target = site_ref[0, order[index]]
-        copy = pltpu.make_async_copy(wide_ref.at[index], out_ref.at[target], sem_ref.at[index])
-        copy.start()
-        copies.append(copy)
+            values = code_ref[source, block * 16 : block * 16 + 16, :].astype(jnp.int32).astype(F32)
+            wide_ref[site, block * 16 : block * 16 + 16, :] = values * scale[block : block + 1]
+        if site % CHUNK == CHUNK - 1:
+            here = pl.ds(site - CHUNK + 1, CHUNK)
+            copy = pltpu.make_async_copy(wide_ref.at[here], out_ref.at[here], sem_ref.at[site // CHUNK])
+            copy.start()
+            copies.append(copy)
     for copy in copies:
         copy.wait()
 
@@ -365,31 +416,32 @@
     )(block)
 
 
-def own_call(own, start, mix, gauge):
+def own_call(face_x, own, start, mix, gauge):
     return pl.pallas_call(
         own_kernel,
         out_shape=[
-            jax.ShapeDtypeStruct((384, 3 * PAD), BF16),
+            jax.ShapeDtypeStruct((256, 3 * PAD), BF16),
             jax.ShapeDtypeStruct((WIDE, 2 * PAD), BF16),
-            jax.ShapeDtypeStruct((128, 4 * PAD), F32),
-            jax.ShapeDtypeStruct((3, WIDE, 256), BF16),
-            jax.ShapeDtypeStruct((96, 48), F32),
-            jax.ShapeDtypeStruct((96, 48), F32),
+            jax.ShapeDtypeStruct((128, 4 * PAD), BF16),
+            jax.ShapeDtypeStruct((2, WIDE, 256), BF16),
+            jax.ShapeDtypeStruct((192, 48), BF16),
+            jax.ShapeDtypeStruct((144, 128), F32),
         ],
+        scratch_shapes=[pltpu.VMEM((192, 48), F32)],
         compiler_params=pltpu.CompilerParams(vmem_limit_bytes=40 * 2**20),
         cost_estimate=pl.CostEstimate(flops=2 * 10**9, bytes_accessed=4 * 10**6, transcendentals=0),
         name="own_part",
-    )(own, start, mix, gauge)
-
-
-def second_call(faces, prepared):
+    )(face_x, own, start, mix, gauge)
+
+
+def second_call(face_y, face_z, prepared):
     return pl.pallas_call(
         second_kernel,
         out_shape=jax.ShapeDtypeStruct((160, 128), jnp.int16),
-        scratch_shapes=[pltpu.VMEM((384, 48), F32), pltpu.VMEM((144, 128), F32)],
+        scratch_shapes=[pltpu.VMEM((192, 48), F32), pltpu.VMEM((144, 128), F32)],
         compiler_params=pltpu.CompilerParams(vmem_limit_bytes=40 * 2**20),
         name="coarse_links",
-    )(*faces, *prepared)
+    )(face_y, face_z, *prepared)
 
 
 def place_call(site_map, codes, order):
@@ -398,7 +450,11 @@
         in_specs=[pl.BlockSpec(memory_space=pltpu.SMEM), pl.BlockSpec(memory_space=pltpu.VMEM)],
         out_specs=pl.BlockSpec(memory_space=pl.ANY),
         out_shape=jax.ShapeDtypeStruct((COUNT, 144, 128), F32),
-        scratch_shapes=[pltpu.VMEM((COUNT, 144, 128), F32), pltpu.SemaphoreType.DMA((COUNT,))],
+        scratch_shapes=[
+            pltpu.VMEM((COUNT, 144, 128), F32),
+            pltpu.SMEM((COUNT,), jnp.int32),
+            pltpu.SemaphoreType.DMA((COUNT // CHUNK,)),
+        ],
         compiler_params=pltpu.CompilerParams(vmem_limit_bytes=40 * 2**20),
         name="place_links",
     )(site_map, codes)
@@ -427,8 +483,8 @@
     face_y = passed_back(face_y, "gy")
     face_x = passed_back(face_x, "gx")
     face_z = passed_back(face_z, "zt")
-    prepared = own_call(own, start, mix, gauge.reshape(2 * SITES, LINKS))
-    code = second_call((face_x, face_y, face_z), prepared)
+    prepared = own_call(face_x, own, start, mix, gauge.reshape(2 * SITES, LINKS))
+    code = second_call(face_y, face_z, prepared)
     codes, order = gathered(code)
     placed = place_call(site_map, codes, order)
     placed = placed.reshape(COUNT, 72, 2, 128).transpose(0, 2, 1, 3)

time: 68.8 us -> 67.1 us (0.975)
  Pallas kernels: 12.2 us -> 10.5 us
    pallas_call x1, Pallas kernels: 3.99 us -> 2.11 us  [second_call(): pl.pallas_call(second_kernel, out_shape=jax.ShapeDtypeStruct((160, 128),...]
  transfers between devices with their start and end apart: 3 -> 3, of which waited for: 0 -> 0; matrix products, arithmetic and copies ran while one was open for 1% -> 1% of each run, Pallas kernels for 3% -> 4%
where the time goes in v4:
time: 67.1 us; the launch traced here: 66.8 us
  blocking collectives  37.4 us (56%)
  starting transfers between devices  16.8 us (25%)
  Pallas kernels  10.5 us (16%)
  local copies, waits for them, and re-layouts  1.98 us (3%)
    all_gather x1, blocking collectives, gathered(): lax.all_gather(code, names, axis=0, tiled=True, axis_index_groups=rings)  33.9 us
    ppermute x3, starting transfers between devices, passed_back(): lax.ppermute(value, axis, [(source, (source - 1) % count) for source in r...  16.8 us
    pallas_call x1, Pallas kernels, first_call(): pl.pallas_call(first_kernel, out_shape=[jax.ShapeDtypeStruct((4, 128, WID...  3.53 us
    all_gather x1, blocking collectives, gathered(): lax.all_gather(code[None], names, axis=0, tiled=True, axis_index_groups=p...  3.53 us
    pallas_call x1, Pallas kernels, own_call(): pl.pallas_call(own_kernel, out_shape=[jax.ShapeDtypeStruct((256, 3 * PAD)...  2.81 us
    pallas_call x1, Pallas kernels, second_call(): pl.pallas_call(second_kernel, out_shape=jax.ShapeDtypeStruct((160, 128),...  2.11 us
    pallas_call x1, Pallas kernels, place_call(): pl.pallas_call(lambda *refs: place_kernel(order, *refs), in_specs=[pl.Blo...  2.09 us
  transfers between devices with their start and end apart: 3, of which 0 were waited for; matrix products, arithmetic and copies ran while one was open for 1% of the time, Pallas kernels for 4%

profile of v4, /device:TPU:1, one launch (start us, length us, event | category | flops | bytes accessed | tf_op | source)
XLA Modules:
  0.0 66.8 jit_solution(10418035347090320072)
XLA Ops:
  0.0 1.1 %reshape.12.nn_ref = bf16[128,1152]{1,0:T(8,128)(2,1)S(1)} reshape(bf16[4,4,4,2,1152]{4,3,2,1,0:T(2,128)(2,1)} %param.3) | data formatting | bytes 589824 | tf_op jit(solution)/shard_map/reshape | solution.py:482
  1.1 3.5 %gram_and_mixing.1 = (bf16[4,128,288]{2,1,0:T(8,128)(2,1)S(1)}, bf16[128,288]{1,0:T(8,128)(2,1)S(1)}, f32[24,128]{1,0:T(8,128)S(1)}, bf16[336,128]{1,0:T(8,128)(...) custom-call(bf16[128,1152]{1,0:T(8,128)(2,1)S(1)} %reshape.12.nn_ref), custom_call_target="tpu_custom_call" | custom-call | tf_op jit(solution)/shard_map/gram_and_mixing/pallas_call | solution.py:406
  4.6 7.1 %collective-permute-start.2 = (bf16[336,128]{1,0:T(8,128)(2,1)S(1)}, bf16[336,128]{1,0:T(8,128)(2,1)S(1)}, u32[]{:S(2)}, u32[]{:S(2)}) collective-permute-start(bf16[336,128]{1,0:T(8,128)(2,1)S(1)} %get-tuple-element.19), channel_id=1, source_target_pairs={{0,384},{128,0},{256,128},{384,256},{1,385},{129,1},{257,129},{385... | collective-permute-start | bytes 258056 | tf_op jit(solution)/shard_map/ppermute | solution.py:465
  11.7 3.6 %collective-permute-start = (bf16[336,128]{1,0:T(8,128)(2,1)S(1)}, bf16[336,128]{1,0:T(8,128)(2,1)S(1)}, u32[]{:S(2)}, u32[]{:S(2)}) collective-permute-start(bf16[336,128]{1,0:T(8,128)(2,1)S(1)} %get-tuple-element.17), channel_id=1, source_target_pairs={{0,112},{16,0},{32,16},{48,32},{64,48},{80,64},{96,80},{112,96},{1... | collective-permute-start | bytes 258056 | tf_op jit(solution)/shard_map/ppermute | solution.py:465
  15.3 6.1 %collective-permute-start.1 = (bf16[336,128]{1,0:T(8,128)(2,1)S(1)}, bf16[336,128]{1,0:T(8,128)(2,1)S(1)}, u32[]{:S(2)}, u32[]{:S(2)}) collective-permute-start(bf16[336,128]{1,0:T(8,128)(2,1)S(1)} %get-tuple-element.18), channel_id=1, source_target_pairs={{0,15},{1,0},{2,1},{3,2},{4,3},{5,4},{6,5},{7,6},{8,7},{9,8},{10,9... | collective-permute-start | bytes 258056 | tf_op jit(solution)/shard_map/ppermute | solution.py:465
  21.4 0.9 %reshape.13.ga_ref = bf16[128,144]{1,0:T(8,128)(2,1)S(1)} reshape(bf16[4,4,4,2,144]{4,3,2,1,0:T(2,128)(2,1)} %param.4) | data formatting | bytes 73728 | tf_op jit(solution)/shard_map/reshape | solution.py:486
  22.3 0.0 collective-permute-done.2.rx_ref
  22.3 2.8 %own_part.1 = (bf16[256,1152]{1,0:T(8,128)(2,1)S(1)}, bf16[288,768]{1,0:T(8,128)(2,1)S(1)}, bf16[128,1536]{1,0:T(8,128)(2,1)S(1)}, bf16[2,288,256]{2,1,0:T(8,128...) custom-call(bf16[336,128]{1,0:T(8,128)(2,1)S(1)} %collective-permute-done.2.rx_ref, ...), custom_call_target="tpu_custom_call" | custom-call | flops 2000000000 | bytes 4000000 | tf_op jit(solution)/shard_map/own_part/pallas_call | solution.py:420
  25.1 0.0 copy-start
  25.2 0.0 collective-permute-done.ry_ref
  25.2 0.0 collective-permute-done.1.rz_ref
  25.2 2.1 %coarse_links.1 = s16[160,128]{1,0:T(8,128)(2,1)S(1)} custom-call(bf16[336,128]{1,0:T(8,128)(2,1)S(1)} %collective-permute-done.ry_ref, bf16[336,128]{1,0:T(8,128)(2,1)S(1)} %collective-permute-done.1.rz_ref, bf16[256,1152]{1,0:T(8,128)(2,1)S(1)} %get-tuple-element.23.gauge_ref, bf16[288,768]{1,0:T(8,128)(2,1)S(1)} %get-tuple-element.24.turns_ref, ...), custom_call_target="tpu_custom_call" | custom-call | tf_op jit(solution)/shard_map/coarse_links/pallas_call | solution.py:438
  27.3 3.5 %all-gather = s16[320,128]{1,0:T(8,128)(2,1)S(1)} all-gather(s16[160,128]{1,0:T(8,128)(2,1)S(1)} %coarse_links.1), channel_id=2, replica_groups={{0,128},{16,144},{256,384},{272,400},{32,160},{48,176},{288,416},{304,4..., dimensions={0}, use_global_device_ids=true | all-gather | bytes 122880 | tf_op jit(solution)/shard_map/all_gather | solution.py:476
  30.8 33.9 %all-gather.2.refs_1_ = s16[32,160,128]{2,1,0:T(8,128)(2,1)S(1)} all-gather(s16[2,160,128]{2,1,0:T(8,128)(2,1)S(1)} %bitcast.6), channel_id=1, replica_groups={{0,16,256,272,32,48,288,304,64,80,320,336,96,112,352,368},{128,144,384,..., dimensions={0}, use_global_device_ids=true | all-gather | bytes 1392640 | tf_op jit(solution)/shard_map/all_gather | solution.py:477
  64.7 0.0 copy-done
  64.7 2.1 %place_links.1 = f32[32,144,128]{2,1,0:T(8,128)} custom-call(s32[1,32]{1,0:T(1,128)S(1)} %copy-done, s16[32,160,128]{2,1,0:T(8,128)(2,1)S(1)} %all-gather.2.refs_1_), custom_call_target="tpu_custom_call" | custom-call | tf_op jit(solution)/shard_map/place_links/pallas_call | solution.py:448
Async XLA Ops:
  4.6 17.7 %collective-permute-start.2 = (bf16[336,128]{1,0:T(8,128)(2,1)S(1)}, bf16[336,128]{1,0:T(8,128)(2,1)S(1)}, u32[]{:S(2)}, u32[]{:S(2)}) collective-permute-start(bf16[336,128]{1,0:T(8,128)(2,1)S(1)} %get-tuple-element.19), channel_id=1, source_target_pairs={{0,384},{128,0},{256,128},{384,256},{1,385},{129,1},{257,129},{385... | collective-permute-start | bytes 258056 | tf_op jit(solution)/shard_map/ppermute | solution.py:465
  11.7 13.5 %collective-permute-start = (bf16[336,128]{1,0:T(8,128)(2,1)S(1)}, bf16[336,128]{1,0:T(8,128)(2,1)S(1)}, u32[]{:S(2)}, u32[]{:S(2)}) collective-permute-start(bf16[336,128]{1,0:T(8,128)(2,1)S(1)} %get-tuple-element.17), channel_id=1, source_target_pairs={{0,112},{16,0},{32,16},{48,32},{64,48},{80,64},{96,80},{112,96},{1... | collective-permute-start | bytes 258056 | tf_op jit(solution)/shard_map/ppermute | solution.py:465
  15.3 9.8 %collective-permute-start.1 = (bf16[336,128]{1,0:T(8,128)(2,1)S(1)}, bf16[336,128]{1,0:T(8,128)(2,1)S(1)}, u32[]{:S(2)}, u32[]{:S(2)}) collective-permute-start(bf16[336,128]{1,0:T(8,128)(2,1)S(1)} %get-tuple-element.18), channel_id=1, source_target_pairs={{0,15},{1,0},{2,1},{3,2},{4,3},{5,4},{6,5},{7,6},{8,7},{9,8},{10,9... | collective-permute-start | bytes 258056 | tf_op jit(solution)/shard_map/ppermute | solution.py:465
  25.1 39.6 %copy-start = (s32[1,32]{1,0:T(1,128)S(1)}, s32[1,32]{1,0:T(1,128)}, u32[]{:S(2)}) copy-start(s32[1,32]{1,0:T(1,128)} %refs_0_.1) | copy-start | bytes 388

commit v5 on v4

--- a/solution.py
+++ b/solution.py
@@ -20,6 +20,7 @@
 CHUNK = 4
 MIX_ROW = 288
 SENT = 336
+ARRIVALS = ("x", "z near", "y early", "z far", "y late")
 TARGET = 64.0
 GAMMA = [
     ((0, 1, -1j), (1, 0, -1j)),
@@ -175,7 +176,7 @@
     return jnp.concatenate(mix, axis=0) * jnp.sqrt(TARGET / weights)
 
 
-def first_kernel(nn_ref, own_ref, start_ref, mix_ref, py_ref, px_ref, pz_ref):
+def first_kernel(nn_ref, own_ref, start_ref, mix_ref, *sent_refs):
     selection = jnp.concatenate(all_rows() + layer_rows(3) + layer_rows(0), axis=0)
     chosen = dot(selection, nn_ref[...]).astype(BF16)
     every = chosen[:128]
@@ -196,8 +197,8 @@
     mix = mixing_rows(hermitian, hermitian_turned)
     mix_ref[...] = mix
     packed = jnp.concatenate(bf16_parts(mix, 2), axis=0)
-    for axis, out in enumerate((px_ref, py_ref, pz_ref)):
-        first = 224 + 32 * axis
+    for name, out in zip(ARRIVALS, sent_refs):
+        first = 224 + 32 * "xyz".index(name[0])
         for column in range(9):
             out[column * 32 : column * 32 + 32, :] = chosen[first : first + 32, column * 128 : (column + 1) * 128]
         out[MIX_ROW:, :] = packed
@@ -281,9 +282,13 @@
     return on[:48, :48] + on[48:, 128:], on[:48, 128:] - on[48:, :48]
 
 
-def next_face(ref):
-    face = jnp.concatenate([ref[column * 32 : column * 32 + 32, :] for column in range(9)], axis=1)
-    parts = ref[MIX_ROW:SENT, :].astype(F32)
+def next_face(*refs):
+    value = refs[0][...].astype(F32)
+    if len(refs) == 2:
+        value = value + refs[1][...].astype(F32)
+    packed = value.astype(BF16)
+    face = jnp.concatenate([packed[column * 32 : column * 32 + 32] for column in range(9)], axis=1)
+    parts = value[MIX_ROW:]
     parts = [parts[:NVEC].astype(BF16), parts[NVEC:].astype(BF16)]
     return jnp.concatenate([time_rows(face[:16]), time_rows(face[16:])], axis=0), parts
 
@@ -302,9 +307,12 @@
                 order_ref[pl.ds(target, 6, stride=6), :] = long[first : first + 6, third * 128 : (third + 1) * 128]
 
 
-def own_kernel(
-    rx_ref, own_ref, start_ref, mix_ref, ga_ref, gauge_ref, turns_ref, spread_ref, rows_ref, left_ref, order_ref, flat_ref
+def prepare_kernel(
+    own_ref, mix_ref, ga_ref, far_ref, late_ref,
+    gauge_ref, turns_ref, spread_ref, rows_ref, left_ref, far_out_ref, late_out_ref,
 ):
+    far_out_ref[...] = far_ref[...]
+    late_out_ref[...] = late_ref[...]
     selection = jnp.concatenate(all_rows() + layer_rows(3), axis=0)
     face_links = dot(selection, ga_ref[...]).astype(BF16)
     picked = dot(face_links, link_pick()).astype(BF16)
@@ -317,11 +325,9 @@
                 link_rows.append(picked[first + 16 * part : first + 16 * part + 16, piece * 128 : piece * 128 + 16])
     link_rows.append(picked[:128, 12 * 128 : 12 * 128 + 16])
     gauge = dot(jnp.concatenate(link_rows, axis=0), link_spread()).astype(BF16)
-    gauge_ref[...] = gauge[128:384]
-    turns = colour_turns()
-    turns_ref[...] = turns
-    spread_matrix = mixing_spread()
-    spread_ref[...] = spread_matrix
+    gauge_ref[...] = gauge
+    turns_ref[...] = colour_turns()
+    spread_ref[...] = mixing_spread()
     mix = mix_ref[...]
     zero = jnp.zeros((NVEC, NVEC), F32)
     left = []
@@ -331,41 +337,44 @@
         left += [jnp.concatenate([first, zero], axis=1), jnp.concatenate([zero, second], axis=1)]
     left = jnp.concatenate(bf16_parts(jnp.concatenate(left, axis=0), 2), axis=0)
     left_ref[...] = left
-    rows = []
     for axis in range(4):
         mine = own_ref[axis]
-        rows.append(jnp.concatenate([mine, mine], axis=0).T)
-    rows_ref[0] = rows[1]
-    rows_ref[1] = rows[2]
+        rows_ref[axis] = jnp.concatenate([mine, mine], axis=0).T
+
+
+def own_kernel(rx_ref, start_ref, mix_ref, gauge_ref, turns_ref, spread_ref, rows_ref, left_ref, order_ref, flat_ref):
+    mix = mix_ref[...]
+    left = left_ref[...]
     face, mix_x = next_face(rx_ref)
     ahead = jnp.concatenate([face, start_ref[...]], axis=0)
-    turned = dot(ahead, turns)
-    mixings = spread_mixing([jnp.concatenate(pair, axis=0) for pair in zip(mix_x, bf16_parts(mix, 2))], spread_matrix)
+    turned = dot(ahead, turns_ref[...])
+    mixings = spread_mixing([jnp.concatenate(pair, axis=0) for pair in zip(mix_x, bf16_parts(mix, 2))], spread_ref[...])
     links = []
     for index, direction in enumerate((0, 3)):
         here = slice(index * 128, index * 128 + 128)
-        to_re, to_im = hop(gauge[direction * 128 : direction * 128 + 128], ahead[here], turned[here], 1.0 - 2.0 * index)
-        folded = spin_fold(dot(rows[direction], to_re), dot(rows[direction], to_im), direction)
+        to_re, to_im = hop(gauge_ref[direction * 128 : direction * 128 + 128, :], ahead[here], turned[here], 1.0 - 2.0 * index)
+        folded = spin_fold(dot(rows_ref[direction], to_re), dot(rows_ref[direction], to_im), direction)
         links.append((direction, *link_matrix(folded, mixings[index], left)))
     order_ref[...] = jnp.zeros((144, 128), F32)
     write_rows(links, flat_ref, order_ref)
 
 
 def second_kernel(
-    ry_ref, rz_ref, gauge_ref, turns_ref, spread_ref, rows_ref, left_ref, start_ref, code_ref, flat_ref, order_ref
+    near_ref, early_ref, far_ref, late_ref, gauge_ref, turns_ref, spread_ref, rows_ref, left_ref, start_ref,
+    code_ref, flat_ref, order_ref,
 ):
     order_ref[...] = start_ref[...]
     left = left_ref[...]
-    face_y, mix_y = next_face(ry_ref)
-    face_z, mix_z = next_face(rz_ref)
+    face_y, mix_y = next_face(early_ref, late_ref)
+    face_z, mix_z = next_face(near_ref, far_ref)
     ahead = jnp.concatenate([face_y, face_z], axis=0)
     turned = dot(ahead, turns_ref[...])
     mixings = spread_mixing([jnp.concatenate(pair, axis=0) for pair in zip(mix_y, mix_z)], spread_ref[...])
     links = []
     for index, direction in enumerate((1, 2)):
         here = slice(index * 128, index * 128 + 128)
-        to_re, to_im = hop(gauge_ref[here, :], ahead[here], turned[here], 1.0)
-        rows = rows_ref[index]
+        to_re, to_im = hop(gauge_ref[direction * 128 : direction * 128 + 128, :], ahead[here], turned[here], 1.0)
+        rows = rows_ref[direction]
         folded = spin_fold(dot(rows, to_re), dot(rows, to_im), direction)
         links.append((direction, *link_matrix(folded, mixings[index], left)))
     write_rows(links, flat_ref, order_ref)
@@ -410,38 +419,49 @@
             jax.ShapeDtypeStruct((128, WIDE), BF16),
             jax.ShapeDtypeStruct((NVEC, 128), F32),
         ]
-        + [jax.ShapeDtypeStruct((SENT, 128), BF16)] * 3,
+        + [jax.ShapeDtypeStruct((SENT, 128), BF16)] * len(ARRIVALS),
         compiler_params=pltpu.CompilerParams(vmem_limit_bytes=40 * 2**20),
         name="gram_and_mixing",
     )(block)
 
 
-def own_call(face_x, own, start, mix, gauge):
+def prepare_call(own, mix, gauge, far, late):
+    return pl.pallas_call(
+        prepare_kernel,
+        out_shape=[
+            jax.ShapeDtypeStruct((512, 3 * PAD), BF16),
+            jax.ShapeDtypeStruct((WIDE, 2 * PAD), BF16),
+            jax.ShapeDtypeStruct((128, 4 * PAD), BF16),
+            jax.ShapeDtypeStruct((4, WIDE, 256), BF16),
+            jax.ShapeDtypeStruct((192, 48), BF16),
+            jax.ShapeDtypeStruct((SENT, 128), BF16),
+            jax.ShapeDtypeStruct((SENT, 128), BF16),
+        ],
+        compiler_params=pltpu.CompilerParams(vmem_limit_bytes=40 * 2**20),
+        cost_estimate=pl.CostEstimate(flops=10**9, bytes_accessed=4 * 10**6, transcendentals=0),
+        name="prepare",
+    )(own, mix, gauge, far, late)
+
+
+def own_call(face_x, start, mix, prepared):
     return pl.pallas_call(
         own_kernel,
-        out_shape=[
-            jax.ShapeDtypeStruct((256, 3 * PAD), BF16),
-            jax.ShapeDtypeStruct((WIDE, 2 * PAD), BF16),
-            jax.ShapeDtypeStruct((128, 4 * PAD), BF16),
-            jax.ShapeDtypeStruct((2, WIDE, 256), BF16),
-            jax.ShapeDtypeStruct((192, 48), BF16),
-            jax.ShapeDtypeStruct((144, 128), F32),
-        ],
+        out_shape=jax.ShapeDtypeStruct((144, 128), F32),
         scratch_shapes=[pltpu.VMEM((192, 48), F32)],
         compiler_params=pltpu.CompilerParams(vmem_limit_bytes=40 * 2**20),
-        cost_estimate=pl.CostEstimate(flops=2 * 10**9, bytes_accessed=4 * 10**6, transcendentals=0),
+        cost_estimate=pl.CostEstimate(flops=10**9, bytes_accessed=4 * 10**6, transcendentals=0),
         name="own_part",
-    )(face_x, own, start, mix, gauge)
-
-
-def second_call(face_y, face_z, prepared):
+    )(face_x, start, mix, *prepared)
+
+
+def second_call(faces, prepared):
     return pl.pallas_call(
         second_kernel,
         out_shape=jax.ShapeDtypeStruct((160, 128), jnp.int16),
         scratch_shapes=[pltpu.VMEM((192, 48), F32), pltpu.VMEM((144, 128), F32)],
         compiler_params=pltpu.CompilerParams(vmem_limit_bytes=40 * 2**20),
         name="coarse_links",
-    )(face_y, face_z, *prepared)
+    )(*faces, *prepared)
 
 
 def place_call(site_map, codes, order):
@@ -460,9 +480,15 @@
     )(site_map, codes)
 
 
-def passed_back(value, axis):
+def passed_back(value, name):
+    axis = {"x": "gx", "y": "gy", "z": "zt"}[name[0]]
+    if axis == "gy":
+        columns = [column for column in range(16) if (column % 4 == 0) == name.endswith("early")]
+        pairs = [(source * 16 + column, (source - 1) % 8 * 16 + column) for source in range(8) for column in columns]
+        return lax.ppermute(value, ("gy", "zt"), pairs)
     count = lax.axis_size(axis)
-    return lax.ppermute(value, axis, [(source, (source - 1) % count) for source in range(count)])
+    sources = [source for source in range(count) if axis == "gx" or (source % 4 == 0) == name.endswith("far")]
+    return lax.ppermute(value, axis, [(source, (source - 1) % count) for source in sources])
 
 
 def flat_index(z, core):
@@ -479,12 +505,13 @@
 
 
 def body(near_null, gauge, site_map):
-    own, start, mix, face_y, face_x, face_z = first_call(near_null.reshape(2 * SITES, FULL))
-    face_y = passed_back(face_y, "gy")
-    face_x = passed_back(face_x, "gx")
-    face_z = passed_back(face_z, "zt")
-    prepared = own_call(face_x, own, start, mix, gauge.reshape(2 * SITES, LINKS))
-    code = second_call(face_y, face_z, prepared)
+    own, start, mix, *faces = first_call(near_null.reshape(2 * SITES, FULL))
+    faces = dict(zip(ARRIVALS, faces))
+    *prepared, faces["z far"], faces["y late"] = prepare_call(
+        own, mix, gauge.reshape(2 * SITES, LINKS), faces["z far"], faces["y late"]
+    )
+    face_x, *faces = [passed_back(faces[name], name) for name in ARRIVALS]
+    code = second_call(faces, [*prepared, own_call(face_x, start, mix, prepared)])
     codes, order = gathered(code)
     placed = place_call(site_map, codes, order)
     placed = placed.reshape(COUNT, 72, 2, 128).transpose(0, 2, 1, 3)

time: 67.1 us -> 67.9 us (1.012)
  starting transfers between devices: 16.8 us -> 17.6 us
    ppermute x3 -> x5, starting transfers between devices: 16.8 us -> 17.6 us  [the longest x2 9.45 us: passed_back(): return lax.ppermute(value, ('gy', 'zt'), pairs)]
    pallas_call x1 -> x2, Pallas kernels: 2.81 us -> 3.08 us  [the longest x1 2.08 us: own_call(): pl.pallas_call(own_kernel, out_shape=jax.ShapeDtypeStruct((144, 128), F32...]
  transfers between devices with their start and end apart: 3 -> 5, of which waited for: 0 -> 0; matrix products, arithmetic and copies ran while one was open for 1% -> 1% of each run, Pallas kernels for 4% -> 5%
where the time goes in v5:
time: 67.9 us; the launch traced here: 67.6 us
  blocking collectives  37.1 us (55%)
  starting transfers between devices  17.6 us (26%)
  Pallas kernels  10.8 us (16%)
  local copies, waits for them, and re-layouts  1.98 us (3%)
    all_gather x1, blocking collectives, gathered(): lax.all_gather(code, names, axis=0, tiled=True, axis_index_groups=rings)  33.5 us
    ppermute x2, starting transfers between devices, passed_back(): return lax.ppermute(value, ('gy', 'zt'), pairs)  9.45 us
    ppermute x3, starting transfers between devices, passed_back(): lax.ppermute(value, axis, [(source, (source - 1) % count) for source in s...  8.17 us
    pallas_call x1, Pallas kernels, first_call(): pl.pallas_call(first_kernel, out_shape=[jax.ShapeDtypeStruct((4, 128, WID...  3.53 us
    all_gather x1, blocking collectives, gathered(): lax.all_gather(code[None], names, axis=0, tiled=True, axis_index_groups=p...  3.53 us
    pallas_call x1, Pallas kernels, second_call(): pl.pallas_call(second_kernel, out_shape=jax.ShapeDtypeStruct((160, 128),...  2.11 us
    pallas_call x1, Pallas kernels, place_call(): pl.pallas_call(lambda *refs: place_kernel(order, *refs), in_specs=[pl.Blo...  2.09 us
    pallas_call x1, Pallas kernels, own_call(): pl.pallas_call(own_kernel, out_shape=jax.ShapeDtypeStruct((144, 128), F32...  2.08 us
  transfers between devices with their start and end apart: 5, of which 0 were waited for; matrix products, arithmetic and copies ran while one was open for 1% of the time, Pallas kernels for 5%

profile of v5, /device:TPU:1, one launch (start us, length us, event | category | flops | bytes accessed | tf_op | source)
XLA Modules:
  0.0 67.6 jit_solution(10960944276135343546)
XLA Ops:
  0.0 1.1 %reshape.12.nn_ref = bf16[128,1152]{1,0:T(8,128)(2,1)S(1)} reshape(bf16[4,4,4,2,1152]{4,3,2,1,0:T(2,128)(2,1)} %param.3) | data formatting | bytes 589824 | tf_op jit(solution)/shard_map/reshape | solution.py:508
  1.1 3.5 %gram_and_mixing.1 = (bf16[4,128,288]{2,1,0:T(8,128)(2,1)S(1)}, bf16[128,288]{1,0:T(8,128)(2,1)S(1)}, f32[24,128]{1,0:T(8,128)S(1)}, bf16[336,128]{1,0:T(8,128)(...) custom-call(bf16[128,1152]{1,0:T(8,128)(2,1)S(1)} %reshape.12.nn_ref), custom_call_target="tpu_custom_call" | custom-call | tf_op jit(solution)/shard_map/gram_and_mixing/pallas_call | solution.py:415
  4.6 1.3 %collective-permute-start = (bf16[336,128]{1,0:T(8,128)(2,1)S(1)}, bf16[336,128]{1,0:T(8,128)(2,1)S(1)}, u32[]{:S(2)}, u32[]{:S(2)}) collective-permute-start(bf16[336,128]{1,0:T(8,128)(2,1)S(1)} %get-tuple-element.20), channel_id=1, source_target_pairs={{1,0},{2,1},{3,2},{5,4},{6,5},{7,6},{9,8},{10,9},{11,10},{13,12},{... | collective-permute-start | bytes 258056 | tf_op jit(solution)/shard_map/ppermute | solution.py:491
  5.9 8.8 %collective-permute-start.1 = (bf16[336,128]{1,0:T(8,128)(2,1)S(1)}, bf16[336,128]{1,0:T(8,128)(2,1)S(1)}, u32[]{:S(2)}, u32[]{:S(2)}) collective-permute-start(bf16[336,128]{1,0:T(8,128)(2,1)S(1)} %get-tuple-element.21), channel_id=1, source_target_pairs={{0,112},{4,116},{8,120},{12,124},{16,0},{20,4},{24,8},{28,12},{32,... | collective-permute-start | bytes 258056 | tf_op jit(solution)/shard_map/ppermute | solution.py:488
  14.7 1.9 %collective-permute-start.4 = (bf16[336,128]{1,0:T(8,128)(2,1)S(1)}, bf16[336,128]{1,0:T(8,128)(2,1)S(1)}, u32[]{:S(2)}, u32[]{:S(2)}) collective-permute-start(bf16[336,128]{1,0:T(8,128)(2,1)S(1)} %get-tuple-element.33), channel_id=1, source_target_pairs={{0,384},{128,0},{256,128},{384,256},{1,385},{129,1},{257,129},{385... | collective-permute-start | bytes 258056 | tf_op jit(solution)/shard_map/ppermute | solution.py:491
  16.6 0.9 %reshape.13.ga_ref = bf16[128,144]{1,0:T(8,128)(2,1)S(1)} reshape(bf16[4,4,4,2,144]{4,3,2,1,0:T(2,128)(2,1)} %param.4) | data formatting | bytes 73728 | tf_op jit(solution)/shard_map/reshape | solution.py:511
  17.5 1.0 %prepare.1 = (bf16[512,1152]{1,0:T(8,128)(2,1)S(1)}, bf16[288,768]{1,0:T(8,128)(2,1)S(1)}, bf16[128,1536]{1,0:T(8,128)(2,1)S(1)}, bf16[4,288,256]{2,1,0:T(8,128)...) custom-call(bf16[4,128,288]{2,1,0:T(8,128)(2,1)S(1)} %get-tuple-element.22.own_re, ...), custom_call_target="tpu_custom_call" | custom-call | flops 1000000000 | bytes 4000000 | tf_op jit(solution)/shard_map/prepare/pallas_call | solution.py:429
  18.5 5.0 %collective-permute-start.2 = (bf16[336,128]{1,0:T(8,128)(2,1)S(1)}, bf16[336,128]{1,0:T(8,128)(2,1)S(1)}, u32[]{:S(2)}, u32[]{:S(2)}) collective-permute-start(bf16[336,128]{1,0:T(8,128)(2,1)S(1)} %get-tuple-element.26), channel_id=1, source_target_pairs={{0,15},{4,3},{8,7},{12,11},{16,31},{20,19},{24,23},{28,27},{32,47}... | collective-permute-start | bytes 258056 | tf_op jit(solution)/shard_map/ppermute | solution.py:491
  23.5 0.7 collective-permute-start.3
  24.2 0.0 collective-permute-done.4.rx_ref
  24.2 2.1 %own_part.1.start_ref = f32[144,128]{1,0:T(8,128)S(1)} custom-call(bf16[336,128]{1,0:T(8,128)(2,1)S(1)} %collective-permute-done.4.rx_ref, bf16[128,288]{1,0:T(8,128)(2,1)S(1)} %get-tuple-element.34.start_ref, f32[24,128]{1,0:T(8,128)S(1)} %get-tuple-element.23.mix_ref, bf16[512,1152]{1,0:T(8,128)(2,1)S(1)} %get-tuple-element.28.gauge_ref, ...), custom_call_target="tpu_custom_call" | custom-call | flops 1000000000 | bytes 4000000 | tf_op jit(solution)/shard_map/own_part/pallas_call | solution.py:447
  26.3 0.0 collective-permute-done.near_ref
  26.3 0.0 collective-permute-done.1.early_ref
  26.3 0.0 collective-permute-done.2.far_ref
  26.3 0.0 collective-permute-done.3.late_ref
  26.3 2.1 %coarse_links.1 = s16[160,128]{1,0:T(8,128)(2,1)S(1)} custom-call(bf16[336,128]{1,0:T(8,128)(2,1)S(1)} %collective-permute-done.near_ref, bf16[336,128]{1,0:T(8,128)(2,1)S(1)} %collective-permute-done.1.early_ref, bf16[336,128]{1,0:T(8,128)(2,1)S(1)} %collective-permute-done.2.far_ref, bf16[336,128]{1,0:T(8,128)(2,1)S(1)} %collective-permute-done.3.late_ref, ...), custom_call_target="tpu_custom_call" | custom-call | tf_op jit(solution)/shard_map/coarse_links/pallas_call | solution.py:458
  28.4 0.0 copy-start
  28.5 3.5 %all-gather = s16[320,128]{1,0:T(8,128)(2,1)S(1)} all-gather(s16[160,128]{1,0:T(8,128)(2,1)S(1)} %coarse_links.1), channel_id=2, replica_groups={{0,128},{16,144},{256,384},{272,400},{32,160},{48,176},{288,416},{304,4..., dimensions={0}, use_global_device_ids=true | all-gather | bytes 122880 | tf_op jit(solution)/shard_map/all_gather | solution.py:502
  32.0 33.5 %all-gather.2.refs_1_ = s16[32,160,128]{2,1,0:T(8,128)(2,1)S(1)} all-gather(s16[2,160,128]{2,1,0:T(8,128)(2,1)S(1)} %bitcast.6), channel_id=1, replica_groups={{0,16,256,272,32,48,288,304,64,80,320,336,96,112,352,368},{128,144,384,..., dimensions={0}, use_global_device_ids=true | all-gather | bytes 1392640 | tf_op jit(solution)/shard_map/all_gather | solution.py:503
  65.5 0.0 copy-done
  65.5 2.1 %place_links.1 = f32[32,144,128]{2,1,0:T(8,128)} custom-call(s32[1,32]{1,0:T(1,128)S(1)} %copy-done, s16[32,160,128]{2,1,0:T(8,128)(2,1)S(1)} %all-gather.2.refs_1_), custom_call_target="tpu_custom_call" | custom-call | tf_op jit(solution)/shard_map/place_links/pallas_call | solution.py:468
Async XLA Ops:
  4.6 21.7 %collective-permute-start = (bf16[336,128]{1,0:T(8,128)(2,1)S(1)}, bf16[336,128]{1,0:T(8,128)(2,1)S(1)}, u32[]{:S(2)}, u32[]{:S(2)}) collective-permute-start(bf16[336,128]{1,0:T(8,128)(2,1)S(1)} %get-tuple-element.20), channel_id=1, source_target_pairs={{1,0},{2,1},{3,2},{5,4},{6,5},{7,6},{9,8},{10,9},{11,10},{13,12},{... | collective-permute-start | bytes 258056 | tf_op jit(solution)/shard_map/ppermute | solution.py:491
  5.9 20.4 %collective-permute-start.1 = (bf16[336,128]{1,0:T(8,128)(2,1)S(1)}, bf16[336,128]{1,0:T(8,128)(2,1)S(1)}, u32[]{:S(2)}, u32[]{:S(2)}) collective-permute-start(bf16[336,128]{1,0:T(8,128)(2,1)S(1)} %get-tuple-element.21), channel_id=1, source_target_pairs={{0,112},{4,116},{8,120},{12,124},{16,0},{20,4},{24,8},{28,12},{32,... | collective-permute-start | bytes 258056 | tf_op jit(solution)/shard_map/ppermute | solution.py:488
  14.7 9.5 %collective-permute-start.4 = (bf16[336,128]{1,0:T(8,128)(2,1)S(1)}, bf16[336,128]{1,0:T(8,128)(2,1)S(1)}, u32[]{:S(2)}, u32[]{:S(2)}) collective-permute-start(bf16[336,128]{1,0:T(8,128)(2,1)S(1)} %get-tuple-element.33), channel_id=1, source_target_pairs={{0,384},{128,0},{256,128},{384,256},{1,385},{129,1},{257,129},{385... | collective-permute-start | bytes 258056 | tf_op jit(solution)/shard_map/ppermute | solution.py:491
  18.5 7.8 %collective-permute-start.2 = (bf16[336,128]{1,0:T(8,128)(2,1)S(1)}, bf16[336,128]{1,0:T(8,128)(2,1)S(1)}, u32[]{:S(2)}, u32[]{:S(2)}) collective-permute-start(bf16[336,128]{1,0:T(8,128)(2,1)S(1)} %get-tuple-element.26), channel_id=1, source_target_pairs={{0,15},{4,3},{8,7},{12,11},{16,31},{20,19},{24,23},{28,27},{32,47}... | collective-permute-start | bytes 258056 | tf_op jit(solution)/shard_map/ppermute | solution.py:491
  23.5 2.8 %collective-permute-start.3 = (bf16[336,128]{1,0:T(8,128)(2,1)S(1)}, bf16[336,128]{1,0:T(8,128)(2,1)S(1)}, u32[]{:S(2)}, u32[]{:S(2)}) collective-permute-start(bf16[336,128]{1,0:T(8,128)(2,1)S(1)} %get-tuple-element.27), channel_id=1, source_target_pairs={{1,113},{2,114},{3,115},{5,117},{6,118},{7,119},{9,121},{10,122},{... | collective-permute-start | bytes 258056 | tf_op jit(solution)/shard_map/ppermute | solution.py:488
  28.4 37.1 %copy-start = (s32[1,32]{1,0:T(1,128)S(1)}, s32[1,32]{1,0:T(1,128)}, u32[]{:S(2)}) copy-start(s32[1,32]{1,0:T(1,128)} %refs_0_.1) | copy-start | bytes 388

commit v6 on v4

--- a/solution.py
+++ b/solution.py
@@ -352,7 +352,7 @@
 
 
 def second_kernel(
-    ry_ref, rz_ref, gauge_ref, turns_ref, spread_ref, rows_ref, left_ref, start_ref, code_ref, flat_ref, order_ref
+    rz_ref, ry_ref, gauge_ref, turns_ref, spread_ref, rows_ref, left_ref, start_ref, code_ref, flat_ref, order_ref
 ):
     order_ref[...] = start_ref[...]
     left = left_ref[...]
@@ -441,7 +441,7 @@
         scratch_shapes=[pltpu.VMEM((192, 48), F32), pltpu.VMEM((144, 128), F32)],
         compiler_params=pltpu.CompilerParams(vmem_limit_bytes=40 * 2**20),
         name="coarse_links",
-    )(face_y, face_z, *prepared)
+    )(face_z, face_y, *prepared)
 
 
 def place_call(site_map, codes, order):

time: 67.1 us -> 67.1 us (level)
  blocking collectives: 37.4 us -> 31.2 us
  waiting for transfers between devices: 0.01 us -> 5.93 us
    all_gather x1, blocking collectives: 33.9 us -> 27.7 us  [gathered(): lax.all_gather(code, names, axis=0, tiled=True, axis_index_groups=rings)]
    ppermute x3, waiting for transfers between devices: 0.01 us -> 5.93 us  [passed_back(): lax.ppermute(value, axis, [(source, (source - 1) % count) for source in r...]
  transfers between devices with their start and end apart: 3 -> 3, of which waited for: 0 -> 1; matrix products, arithmetic and copies ran while one was open for 1% -> 1% of each run, Pallas kernels for 4% -> 4%
where the time goes in v6:
time: 67.1 us; the launch traced here: 66.8 us
  blocking collectives  31.2 us (46%)
  starting transfers between devices  17.1 us (25%)
  Pallas kernels  10.5 us (16%)
  waiting for transfers between devices  5.93 us (9%)
  local copies, waits for them, and re-layouts  1.98 us (3%)
    all_gather x1, blocking collectives, gathered(): lax.all_gather(code, names, axis=0, tiled=True, axis_index_groups=rings)  27.7 us
    ppermute x3, starting transfers between devices, passed_back(): lax.ppermute(value, axis, [(source, (source - 1) % count) for source in r...  17.1 us
    ppermute x3, waiting for transfers between devices, passed_back(): lax.ppermute(value, axis, [(source, (source - 1) % count) for source in r...  5.93 us
    pallas_call x1, Pallas kernels, first_call(): pl.pallas_call(first_kernel, out_shape=[jax.ShapeDtypeStruct((4, 128, WID...  3.53 us
    all_gather x1, blocking collectives, gathered(): lax.all_gather(code[None], names, axis=0, tiled=True, axis_index_groups=p...  3.53 us
    pallas_call x1, Pallas kernels, own_call(): pl.pallas_call(own_kernel, out_shape=[jax.ShapeDtypeStruct((256, 3 * PAD)...  2.81 us
    pallas_call x1, Pallas kernels, second_call(): pl.pallas_call(second_kernel, out_shape=jax.ShapeDtypeStruct((160, 128),...  2.11 us
    pallas_call x1, Pallas kernels, place_call(): pl.pallas_call(lambda *refs: place_kernel(order, *refs), in_specs=[pl.Blo...  2.09 us
  transfers between devices with their start and end apart: 3, of which 1 were waited for; matrix products, arithmetic and copies ran while one was open for 1% of the time, Pallas kernels for 4%

profile of v6, /device:TPU:1, one launch (start us, length us, event | category | flops | bytes accessed | tf_op | source)
XLA Modules:
  0.0 66.8 jit_solution(7946199690736831586)
XLA Ops:
  0.0 1.1 %reshape.12.nn_ref = bf16[128,1152]{1,0:T(8,128)(2,1)S(1)} reshape(bf16[4,4,4,2,1152]{4,3,2,1,0:T(2,128)(2,1)} %param.3) | data formatting | bytes 589824 | tf_op jit(solution)/shard_map/reshape | solution.py:482
  1.1 3.5 %gram_and_mixing.1 = (bf16[4,128,288]{2,1,0:T(8,128)(2,1)S(1)}, bf16[128,288]{1,0:T(8,128)(2,1)S(1)}, f32[24,128]{1,0:T(8,128)S(1)}, bf16[336,128]{1,0:T(8,128)(...) custom-call(bf16[128,1152]{1,0:T(8,128)(2,1)S(1)} %reshape.12.nn_ref), custom_call_target="tpu_custom_call" | custom-call | tf_op jit(solution)/shard_map/gram_and_mixing/pallas_call | solution.py:406
  4.6 7.1 %collective-permute-start.2 = (bf16[336,128]{1,0:T(8,128)(2,1)S(1)}, bf16[336,128]{1,0:T(8,128)(2,1)S(1)}, u32[]{:S(2)}, u32[]{:S(2)}) collective-permute-start(bf16[336,128]{1,0:T(8,128)(2,1)S(1)} %get-tuple-element.19), channel_id=1, source_target_pairs={{0,384},{128,0},{256,128},{384,256},{1,385},{129,1},{257,129},{385... | collective-permute-start | bytes 258056 | tf_op jit(solution)/shard_map/ppermute | solution.py:465
  11.7 6.8 %collective-permute-start = (bf16[336,128]{1,0:T(8,128)(2,1)S(1)}, bf16[336,128]{1,0:T(8,128)(2,1)S(1)}, u32[]{:S(2)}, u32[]{:S(2)}) collective-permute-start(bf16[336,128]{1,0:T(8,128)(2,1)S(1)} %get-tuple-element.17), channel_id=1, source_target_pairs={{0,15},{1,0},{2,1},{3,2},{4,3},{5,4},{6,5},{7,6},{8,7},{9,8},{10,9... | collective-permute-start | bytes 258056 | tf_op jit(solution)/shard_map/ppermute | solution.py:465
  18.5 3.1 %collective-permute-start.1 = (bf16[336,128]{1,0:T(8,128)(2,1)S(1)}, bf16[336,128]{1,0:T(8,128)(2,1)S(1)}, u32[]{:S(2)}, u32[]{:S(2)}) collective-permute-start(bf16[336,128]{1,0:T(8,128)(2,1)S(1)} %get-tuple-element.18), channel_id=1, source_target_pairs={{0,112},{16,0},{32,16},{48,32},{64,48},{80,64},{96,80},{112,96},{1... | collective-permute-start | bytes 258056 | tf_op jit(solution)/shard_map/ppermute | solution.py:465
  21.7 0.9 %reshape.13.ga_ref = bf16[128,144]{1,0:T(8,128)(2,1)S(1)} reshape(bf16[4,4,4,2,144]{4,3,2,1,0:T(2,128)(2,1)} %param.4) | data formatting | bytes 73728 | tf_op jit(solution)/shard_map/reshape | solution.py:486
  22.6 0.0 collective-permute-done.2.rx_ref
  22.6 2.8 %own_part.1 = (bf16[256,1152]{1,0:T(8,128)(2,1)S(1)}, bf16[288,768]{1,0:T(8,128)(2,1)S(1)}, bf16[128,1536]{1,0:T(8,128)(2,1)S(1)}, bf16[2,288,256]{2,1,0:T(8,128...) custom-call(bf16[336,128]{1,0:T(8,128)(2,1)S(1)} %collective-permute-done.2.rx_ref, ...), custom_call_target="tpu_custom_call" | custom-call | flops 2000000000 | bytes 4000000 | tf_op jit(solution)/shard_map/own_part/pallas_call | solution.py:420
  25.4 0.0 copy-start
  25.4 0.0 collective-permute-done.rz_ref
  25.4 5.9 %collective-permute-done.1.ry_ref = bf16[336,128]{1,0:T(8,128)(2,1)S(1)} collective-permute-done((bf16[336,128]{1,0:T(8,128)(2,1)S(1)}, bf16[336,128]{1,0:T(8,128)(2,1)S(1)}, u32[]{:S(2)}, u32[]{:S(2)}) %collective-permute-start.1) | collective-permute-done | bytes 86048 | tf_op jit(solution)/shard_map/ppermute | solution.py:465
  31.4 2.1 %coarse_links.1 = s16[160,128]{1,0:T(8,128)(2,1)S(1)} custom-call(bf16[336,128]{1,0:T(8,128)(2,1)S(1)} %collective-permute-done.rz_ref, bf16[336,128]{1,0:T(8,128)(2,1)S(1)} %collective-permute-done.1.ry_ref, bf16[256,1152]{1,0:T(8,128)(2,1)S(1)} %get-tuple-element.23.gauge_ref, bf16[288,768]{1,0:T(8,128)(2,1)S(1)} %get-tuple-element.24.turns_ref, ...), custom_call_target="tpu_custom_call" | custom-call | tf_op jit(solution)/shard_map/coarse_links/pallas_call | solution.py:438
  33.5 3.5 %all-gather = s16[320,128]{1,0:T(8,128)(2,1)S(1)} all-gather(s16[160,128]{1,0:T(8,128)(2,1)S(1)} %coarse_links.1), channel_id=2, replica_groups={{0,128},{16,144},{256,384},{272,400},{32,160},{48,176},{288,416},{304,4..., dimensions={0}, use_global_device_ids=true | all-gather | bytes 122880 | tf_op jit(solution)/shard_map/all_gather | solution.py:476
  37.0 27.7 %all-gather.2.refs_1_ = s16[32,160,128]{2,1,0:T(8,128)(2,1)S(1)} all-gather(s16[2,160,128]{2,1,0:T(8,128)(2,1)S(1)} %bitcast.6), channel_id=1, replica_groups={{0,16,256,272,32,48,288,304,64,80,320,336,96,112,352,368},{128,144,384,..., dimensions={0}, use_global_device_ids=true | all-gather | bytes 1392640 | tf_op jit(solution)/shard_map/all_gather | solution.py:477
  64.7 0.0 copy-done
  64.7 2.1 %place_links.1 = f32[32,144,128]{2,1,0:T(8,128)} custom-call(s32[1,32]{1,0:T(1,128)S(1)} %copy-done, s16[32,160,128]{2,1,0:T(8,128)(2,1)S(1)} %all-gather.2.refs_1_), custom_call_target="tpu_custom_call" | custom-call | tf_op jit(solution)/shard_map/place_links/pallas_call | solution.py:448
Async XLA Ops:
  4.6 18.0 %collective-permute-start.2 = (bf16[336,128]{1,0:T(8,128)(2,1)S(1)}, bf16[336,128]{1,0:T(8,128)(2,1)S(1)}, u32[]{:S(2)}, u32[]{:S(2)}) collective-permute-start(bf16[336,128]{1,0:T(8,128)(2,1)S(1)} %get-tuple-element.19), channel_id=1, source_target_pairs={{0,384},{128,0},{256,128},{384,256},{1,385},{129,1},{257,129},{385... | collective-permute-start | bytes 258056 | tf_op jit(solution)/shard_map/ppermute | solution.py:465
  11.7 13.7 %collective-permute-start = (bf16[336,128]{1,0:T(8,128)(2,1)S(1)}, bf16[336,128]{1,0:T(8,128)(2,1)S(1)}, u32[]{:S(2)}, u32[]{:S(2)}) collective-permute-start(bf16[336,128]{1,0:T(8,128)(2,1)S(1)} %get-tuple-element.17), channel_id=1, source_target_pairs={{0,15},{1,0},{2,1},{3,2},{4,3},{5,4},{6,5},{7,6},{8,7},{9,8},{10,9... | collective-permute-start | bytes 258056 | tf_op jit(solution)/shard_map/ppermute | solution.py:465
  18.5 12.8 %collective-permute-start.1 = (bf16[336,128]{1,0:T(8,128)(2,1)S(1)}, bf16[336,128]{1,0:T(8,128)(2,1)S(1)}, u32[]{:S(2)}, u32[]{:S(2)}) collective-permute-start(bf16[336,128]{1,0:T(8,128)(2,1)S(1)} %get-tuple-element.18), channel_id=1, source_target_pairs={{0,112},{16,0},{32,16},{48,32},{64,48},{80,64},{96,80},{112,96},{1... | collective-permute-start | bytes 258056 | tf_op jit(solution)/shard_map/ppermute | solution.py:465
  25.4 39.3 %copy-start = (s32[1,32]{1,0:T(1,128)S(1)}, s32[1,32]{1,0:T(1,128)}, u32[]{:S(2)}) copy-start(s32[1,32]{1,0:T(1,128)} %refs_0_.1) | copy-start | bytes 388
